TPU v7x, 32 devices: a whole 2x2x4 slice. The times are simulated.
32 devices in a mesh: rows: 8 (over z, x), cols: 4 (over y, core).
Axes of the slice: x: 2, y: 2, z: 4, core: 2. Of those that a mesh axis runs over, the one named last changes fastest.
Arguments:
- a_tiles: bfloat16 [2304, 7, 128, 128], P(('rows', 'cols')), may hold values from -0.5 to 0.5
- a_cols: int32 [2304, 7], P(('rows', 'cols')), may hold values from 0 to 103, as said below
- ap_slot: int32 [2304, 7, 2], P(('rows', 'cols')), may hold values from 0 to 3
- p_tiles: bfloat16 [2304, 2, 128, 128], P(('rows', 'cols')), may hold values from -0.5 to 0.5
- p_aggs: int32 [2304, 2], P(('rows', 'cols')), may hold values from 0 to 127, as said below
- z_slot: int32 [2304, 2, 4], P(('rows', 'cols')), may hold values from 0 to 15
- send_rows: int32 [32, 4, 8], P(('rows', 'cols')), may hold values from 0 to 71
Outputs:
- coarse: float32 [128, 16, 128, 128], P(('rows', 'cols'))
Inputs may be any that keep to these rules, and one draw needn't show every extreme that they name: `a_cols`: values below 72 are rows of the same device; a value v above names row send_rows[e, q, w % 8] with w = v - 72, q = w // 8 and e the fine row's neighbour in direction q, which always exists. `p_aggs`: column 0 names a coarse row of the fine row's own device; column 1 a coarse row of a device with the same cols index whose rows index differs by at most one; of one device's fine rows at most 9 have column 1 on one neighbouring rows index, and exactly 9 for some device.
All inputs are finite; a program needn't handle non-finite values.
Results may differ from a plain program's by a relative error of at most 0.0041.
Values may be sent and summed in bfloat16 or wider, within the bound.
A program may use at most 192 MiB of HBM per device.

v0:
```python
import math

import jax
import jax.numpy as jnp
from jax import lax
from jax.sharding import PartitionSpec as P

COARSE_SLOTS = 16
CR_DEV = 4


def passed_along(block, axis, distance):
    devices = range(lax.axis_size(axis))
    route = [(i - distance, i) for i in devices if i - distance in devices]
    return lax.ppermute(block, axis, route)


def local(a_tiles, a_cols, ap_slot, p_tiles, p_aggs, z_slot, send_rows):
    rows_here = a_tiles.shape[0]
    tile_size = a_tiles.shape[2]
    slot_count = z_slot.shape[2]
    tile_area = tile_size * tile_size
    col_devices = lax.axis_size("cols")
    send_list = send_rows[0]
    sending = p_tiles[send_list]
    from_rows = [
        passed_along(sending[which], "rows", step_by) for which, step_by in ((0, 1), (1, -1))
    ]
    from_cols = [
        passed_along(sending[which], "cols", step_by) for which, step_by in ((2, 1), (3, -1))
    ]
    arrived = jnp.stack(from_rows + from_cols, 0)
    buffer = jnp.concatenate([p_tiles, arrived.reshape((-1,) + p_tiles.shape[1:])], 0)
    block_rows = math.gcd(rows_here, 8)
    block_count = rows_here // block_rows

    def one_block(block_parts):
        a_part, col_part, slot_part, p_part = block_parts
        gathered = buffer[col_part]
        product = jnp.einsum(
            "rkab,rklbc->rklac", a_part, gathered, preferred_element_type=jnp.float32
        )
        pieces = []
        for slot_value in range(slot_count):
            masked = jnp.where((slot_part == slot_value)[..., None, None], product, 0.0)
            pieces.append(jnp.sum(masked, axis=(1, 2)))
        strip = jnp.stack(pieces, 1).astype(jnp.bfloat16)
        return jnp.einsum(
            "rjba,rsbc->rjsac", p_part, strip, preferred_element_type=jnp.float32
        ).astype(jnp.bfloat16)

    folded = lax.map(
        one_block,
        (
            a_tiles.reshape((block_count, block_rows) + a_tiles.shape[1:]),
            a_cols.reshape((block_count, block_rows) + a_cols.shape[1:]),
            ap_slot.reshape((block_count, block_rows) + ap_slot.shape[1:]),
            p_tiles.reshape((block_count, block_rows) + p_tiles.shape[1:]),
        ),
    )
    by_tile_row = folded.reshape(rows_here * 2, slot_count * tile_area)
    index_local = p_aggs % CR_DEV
    row_tags = index_local[:, :, None] * COARSE_SLOTS + z_slot
    target_row = p_aggs[:, 1] // CR_DEV // col_devices
    moves = target_row - lax.axis_index("rows")
    capacity = max(2, rows_here // 8)
    row_order = jnp.arange(rows_here)
    earlier = (moves[None, :] == moves[:, None]) & (row_order[None, :] < row_order[:, None])
    slot_rank = jnp.sum(earlier.astype(jnp.int32), axis=1)
    tag_range = jnp.arange(CR_DEV * COARSE_SLOTS)
    second_mark = jnp.arange(2) == 1
    own_tags = jnp.where(moves[:, None] == 0, row_tags[:, 1], -1)
    local_labels = jnp.stack([row_tags[:, 0], own_tags], 1).reshape(-1)
    local_select = (local_labels[None, :] == tag_range[:, None]).astype(jnp.bfloat16)
    coarse = jnp.dot(
        local_select,
        by_tile_row.reshape(rows_here * 2 * slot_count, tile_area),
        preferred_element_type=jnp.float32,
    )
    for sign, step_by in ((1, 1), (-1, -1)):
        picker = (moves[None, :] == sign) & (slot_rank[None, :] == jnp.arange(capacity)[:, None])
        picker_wide = (
            (picker[:, :, None] & second_mark[None, None, :])
            .astype(jnp.bfloat16)
            .reshape(capacity, rows_here * 2)
        )
        outbox = jnp.dot(picker_wide, by_tile_row, preferred_element_type=jnp.float32).astype(
            jnp.bfloat16
        )
        outbox = outbox.reshape(capacity, slot_count, tile_size, tile_size)
        filled = jnp.any(picker, axis=1)
        chosen_tags = jnp.sum(
            picker.astype(jnp.int32)[:, :, None] * row_tags[None, :, 1, :], axis=1
        )
        out_tags = jnp.where(filled[:, None], chosen_tags, -1)
        got_terms, got_tags = passed_along((outbox, out_tags), "rows", step_by)
        got_select = (got_tags.reshape(-1)[None, :] == tag_range[:, None]).astype(jnp.bfloat16)
        coarse = coarse + jnp.dot(
            got_select, got_terms.reshape(-1, tile_area), preferred_element_type=jnp.float32
        )
    return coarse.reshape(CR_DEV, COARSE_SLOTS, tile_size, tile_size)


def solution(mesh):
    placed = (
        P(("rows", "cols"), None, None, None),
        P(("rows", "cols"), None),
        P(("rows", "cols"), None, None),
        P(("rows", "cols"), None, None, None),
        P(("rows", "cols"), None),
        P(("rows", "cols"), None, None),
        P(("rows", "cols"), None, None),
    )
    return jax.shard_map(
        local,
        mesh=mesh,
        in_specs=placed,
        out_specs=P(("rows", "cols"), None, None, None),
        check_vma=False,
    )
```

profile of v0, /device:TPU:13, one launch (start us, length us, event | category | flops | bytes accessed | tf_op | source)
XLA Modules:
  0.0 326.7 jit_solution(1734810127791696656)
XLA Ops:
  0.8 3.3 %gather_fusion.1 = bf16[32,2,128,128]{3,2,1,0:T(8,128)(2,1)S(1)} fusion(bf16[72,2,128,128]{3,2,1,0:T(8,128)(2,1)} %param.12, s32[1024]{0:T(1024)S(1)} %pad_clamp_fusion.1), kind=kCustom, calls=%fused_computation.1 | custom fusion | bytes 4194432 | tf_op jit(solution)/shard_map/gather | solution.py:25
  9.2 3.0 collective-permute-start.1
  15.4 4.0 %collective-permute-start.4 = (s32[9,4]{1,0:T(8,128)S(1)}, s32[9,4]{1,0:T(8,128)S(1)}, u32[]{:S(2)}, u32[]{:S(2)}) collective-permute-start(s32[9,4]{1,0:T(8,128)S(1)} %broadcast_select_fusion.1), channel_id=1, source_target_pairs={{0,4},{4,8},{8,12},{12,16},{16,20},{20,24},{24,28},{1,5},{5,9},{9,... | collective-permute-start | bytes 440 | tf_op jit(solution)/shard_map/ppermute | solution.py:15
  20.4 15.9 %collective-permute-done.4 = s32[9,4]{1,0:T(8,128)S(1)} collective-permute-done((s32[9,4]{1,0:T(8,128)S(1)}, s32[9,4]{1,0:T(8,128)S(1)}, u32[]{:S(2)}, u32[]{:S(2)}) %collective-permute-start.4) | collective-permute-done | bytes 176 | tf_op jit(solution)/shard_map/ppermute | solution.py:15
  36.3 4.0 %collective-permute-start.6 = (s32[9,4]{1,0:T(8,128)S(1)}, s32[9,4]{1,0:T(8,128)S(1)}, u32[]{:S(2)}, u32[]{:S(2)}) collective-permute-start(s32[9,4]{1,0:T(8,128)S(1)} %broadcast_select_fusion), channel_id=1, source_target_pairs={{4,0},{8,4},{12,8},{16,12},{20,16},{24,20},{28,24},{5,1},{9,5},{13... | collective-permute-start | bytes 440 | tf_op jit(solution)/shard_map/ppermute | solution.py:15
  41.8 5.7 %pad_maximum_fusion = bf16[104,2,128,128]{3,2,1,0:T(8,128)(2,1)} fusion(bf16[32,2,128,128]{3,2,1,0:T(8,128)(2,1)S(1)} %bitcast.154, bf16[72,2,128,128]{3,2,1,0:T(8,128)(2,1)} %param.12), kind=kLoop, calls=%fused_computation.41 | loop fusion | flops 3407872 | bytes 13631488 | tf_op jit(solution)/shard_map/concatenate | solution.py:33
  47.5 185.4 %while.10 = (s32[]{:T(128)}, bf16[9,8,2,4,128,128]{5,4,3,2,1,0:T(8,128)(2,1)}, s32[9,8,7,2]{1,0,3,2:T(8,128)S(1)}, s32[9,8,7]{1,0,2:T(8,128)S(1)}, bf16[104,2,12...) while((s32[]{:T(128)}, ...), condition=%wide.region_5.6_spmd, body=%wide.region_0.5_spmd.sunk | while | flops 757597824 | bytes 25962288 | solution.py:52
  48.4 5.8 %gather_fusion = bf16[56,2,128,128]{3,2,1,0:T(8,128)(2,1)} fusion(bf16[104,2,128,128]{3,2,1,0:T(8,128)(2,1)} %get-tuple-element.188, s32[1024]{0:T(1024)S(1)} %pad_clamp_fusion.3), kind=kCustom, calls=%fused_computation.clone.1 | custom fusion | bytes 7340256 | tf_op jit(solution)/shard_map/while/body/eval_jaxpr/gather | solution.py:39
  54.2 6.2 %select_reduce_fusion.5 = (bf16[8,128,128]{2,1,0:T(8,128)(2,1)S(1)}, bf16[8,128,128]{2,1,0:T(8,128)(2,1)S(1)}, bf16[8,128,128]{2,1,0:T(8,128)(2,1)S(1)}, bf16[8,128,128]{2,1,0:T(8,128)(2,1)S(1)}) fusion(pred[8,7,2]{2,1,0:T(8,128)(4,1)S(1)} %copy.77, pred[8,7,2]{2,1,0:T(8,128)(4,1)S(1)} %copy.78, pred[8,7,2]{2,1,0:T(8,128)(4,1)S(1)} %copy.79, ...), kind=kOutput, calls=%fused_computation.5.clone.1 | convolution fusion | flops 483917824 | bytes 6554052 | tf_op jit(solution)/shard_map/while/body/eval_jaxpr/rkab,rklbc->rklac/dot_general | solution.py:40
  60.5 3.1 convert_bitcast_fusion.6
  63.6 3.0 copy.82
  69.0 5.8 %gather_fusion = bf16[56,2,128,128]{3,2,1,0:T(8,128)(2,1)} fusion(bf16[104,2,128,128]{3,2,1,0:T(8,128)(2,1)} %get-tuple-element.188, s32[1024]{0:T(1024)S(1)} %pad_clamp_fusion.3), kind=kCustom, calls=%fused_computation.clone.1 | custom fusion | bytes 7340256 | tf_op jit(solution)/shard_map/while/body/eval_jaxpr/gather | solution.py:39
  74.9 6.2 %select_reduce_fusion.5 = (bf16[8,128,128]{2,1,0:T(8,128)(2,1)S(1)}, bf16[8,128,128]{2,1,0:T(8,128)(2,1)S(1)}, bf16[8,128,128]{2,1,0:T(8,128)(2,1)S(1)}, bf16[8,128,128]{2,1,0:T(8,128)(2,1)S(1)}) fusion(pred[8,7,2]{2,1,0:T(8,128)(4,1)S(1)} %copy.77, pred[8,7,2]{2,1,0:T(8,128)(4,1)S(1)} %copy.78, pred[8,7,2]{2,1,0:T(8,128)(4,1)S(1)} %copy.79, ...), kind=kOutput, calls=%fused_computation.5.clone.1 | convolution fusion | flops 483917824 | bytes 6554052 | tf_op jit(solution)/shard_map/while/body/eval_jaxpr/rkab,rklbc->rklac/dot_general | solution.py:40
  81.1 3.1 convert_bitcast_fusion.6
  84.2 3.0 copy.82
  89.6 5.8 %gather_fusion = bf16[56,2,128,128]{3,2,1,0:T(8,128)(2,1)} fusion(bf16[104,2,128,128]{3,2,1,0:T(8,128)(2,1)} %get-tuple-element.188, s32[1024]{0:T(1024)S(1)} %pad_clamp_fusion.3), kind=kCustom, calls=%fused_computation.clone.1 | custom fusion | bytes 7340256 | tf_op jit(solution)/shard_map/while/body/eval_jaxpr/gather | solution.py:39
  95.4 6.2 %select_reduce_fusion.5 = (bf16[8,128,128]{2,1,0:T(8,128)(2,1)S(1)}, bf16[8,128,128]{2,1,0:T(8,128)(2,1)S(1)}, bf16[8,128,128]{2,1,0:T(8,128)(2,1)S(1)}, bf16[8,128,128]{2,1,0:T(8,128)(2,1)S(1)}) fusion(pred[8,7,2]{2,1,0:T(8,128)(4,1)S(1)} %copy.77, pred[8,7,2]{2,1,0:T(8,128)(4,1)S(1)} %copy.78, pred[8,7,2]{2,1,0:T(8,128)(4,1)S(1)} %copy.79, ...), kind=kOutput, calls=%fused_computation.5.clone.1 | convolution fusion | flops 483917824 | bytes 6554052 | tf_op jit(solution)/shard_map/while/body/eval_jaxpr/rkab,rklbc->rklac/dot_general | solution.py:40
  101.7 3.1 convert_bitcast_fusion.6
  104.7 3.0 copy.82
  110.1 5.8 %gather_fusion = bf16[56,2,128,128]{3,2,1,0:T(8,128)(2,1)} fusion(bf16[104,2,128,128]{3,2,1,0:T(8,128)(2,1)} %get-tuple-element.188, s32[1024]{0:T(1024)S(1)} %pad_clamp_fusion.3), kind=kCustom, calls=%fused_computation.clone.1 | custom fusion | bytes 7340256 | tf_op jit(solution)/shard_map/while/body/eval_jaxpr/gather | solution.py:39
  116.0 6.2 %select_reduce_fusion.5 = (bf16[8,128,128]{2,1,0:T(8,128)(2,1)S(1)}, bf16[8,128,128]{2,1,0:T(8,128)(2,1)S(1)}, bf16[8,128,128]{2,1,0:T(8,128)(2,1)S(1)}, bf16[8,128,128]{2,1,0:T(8,128)(2,1)S(1)}) fusion(pred[8,7,2]{2,1,0:T(8,128)(4,1)S(1)} %copy.77, pred[8,7,2]{2,1,0:T(8,128)(4,1)S(1)} %copy.78, pred[8,7,2]{2,1,0:T(8,128)(4,1)S(1)} %copy.79, ...), kind=kOutput, calls=%fused_computation.5.clone.1 | convolution fusion | flops 483917824 | bytes 6554052 | tf_op jit(solution)/shard_map/while/body/eval_jaxpr/rkab,rklbc->rklac/dot_general | solution.py:40
  122.2 3.1 convert_bitcast_fusion.6
  125.3 3.0 copy.82
  130.8 5.8 %gather_fusion = bf16[56,2,128,128]{3,2,1,0:T(8,128)(2,1)} fusion(bf16[104,2,128,128]{3,2,1,0:T(8,128)(2,1)} %get-tuple-element.188, s32[1024]{0:T(1024)S(1)} %pad_clamp_fusion.3), kind=kCustom, calls=%fused_computation.clone.1 | custom fusion | bytes 7340256 | tf_op jit(solution)/shard_map/while/body/eval_jaxpr/gather | solution.py:39
  136.6 6.2 %select_reduce_fusion.5 = (bf16[8,128,128]{2,1,0:T(8,128)(2,1)S(1)}, bf16[8,128,128]{2,1,0:T(8,128)(2,1)S(1)}, bf16[8,128,128]{2,1,0:T(8,128)(2,1)S(1)}, bf16[8,128,128]{2,1,0:T(8,128)(2,1)S(1)}) fusion(pred[8,7,2]{2,1,0:T(8,128)(4,1)S(1)} %copy.77, pred[8,7,2]{2,1,0:T(8,128)(4,1)S(1)} %copy.78, pred[8,7,2]{2,1,0:T(8,128)(4,1)S(1)} %copy.79, ...), kind=kOutput, calls=%fused_computation.5.clone.1 | convolution fusion | flops 483917824 | bytes 6554052 | tf_op jit(solution)/shard_map/while/body/eval_jaxpr/rkab,rklbc->rklac/dot_general | solution.py:40
  142.8 3.1 convert_bitcast_fusion.6
  145.9 3.0 copy.82
  151.4 5.8 %gather_fusion = bf16[56,2,128,128]{3,2,1,0:T(8,128)(2,1)} fusion(bf16[104,2,128,128]{3,2,1,0:T(8,128)(2,1)} %get-tuple-element.188, s32[1024]{0:T(1024)S(1)} %pad_clamp_fusion.3), kind=kCustom, calls=%fused_computation.clone.1 | custom fusion | bytes 7340256 | tf_op jit(solution)/shard_map/while/body/eval_jaxpr/gather | solution.py:39
  157.2 6.2 %select_reduce_fusion.5 = (bf16[8,128,128]{2,1,0:T(8,128)(2,1)S(1)}, bf16[8,128,128]{2,1,0:T(8,128)(2,1)S(1)}, bf16[8,128,128]{2,1,0:T(8,128)(2,1)S(1)}, bf16[8,128,128]{2,1,0:T(8,128)(2,1)S(1)}) fusion(pred[8,7,2]{2,1,0:T(8,128)(4,1)S(1)} %copy.77, pred[8,7,2]{2,1,0:T(8,128)(4,1)S(1)} %copy.78, pred[8,7,2]{2,1,0:T(8,128)(4,1)S(1)} %copy.79, ...), kind=kOutput, calls=%fused_computation.5.clone.1 | convolution fusion | flops 483917824 | bytes 6554052 | tf_op jit(solution)/shard_map/while/body/eval_jaxpr/rkab,rklbc->rklac/dot_general | solution.py:40
  163.5 3.1 convert_bitcast_fusion.6
  166.6 3.0 copy.82
  172.0 5.8 %gather_fusion = bf16[56,2,128,128]{3,2,1,0:T(8,128)(2,1)} fusion(bf16[104,2,128,128]{3,2,1,0:T(8,128)(2,1)} %get-tuple-element.188, s32[1024]{0:T(1024)S(1)} %pad_clamp_fusion.3), kind=kCustom, calls=%fused_computation.clone.1 | custom fusion | bytes 7340256 | tf_op jit(solution)/shard_map/while/body/eval_jaxpr/gather | solution.py:39
  177.8 6.2 %select_reduce_fusion.5 = (bf16[8,128,128]{2,1,0:T(8,128)(2,1)S(1)}, bf16[8,128,128]{2,1,0:T(8,128)(2,1)S(1)}, bf16[8,128,128]{2,1,0:T(8,128)(2,1)S(1)}, bf16[8,128,128]{2,1,0:T(8,128)(2,1)S(1)}) fusion(pred[8,7,2]{2,1,0:T(8,128)(4,1)S(1)} %copy.77, pred[8,7,2]{2,1,0:T(8,128)(4,1)S(1)} %copy.78, pred[8,7,2]{2,1,0:T(8,128)(4,1)S(1)} %copy.79, ...), kind=kOutput, calls=%fused_computation.5.clone.1 | convolution fusion | flops 483917824 | bytes 6554052 | tf_op jit(solution)/shard_map/while/body/eval_jaxpr/rkab,rklbc->rklac/dot_general | solution.py:40
  184.0 3.1 convert_bitcast_fusion.6
  187.1 3.0 copy.82
  192.6 5.8 %gather_fusion = bf16[56,2,128,128]{3,2,1,0:T(8,128)(2,1)} fusion(bf16[104,2,128,128]{3,2,1,0:T(8,128)(2,1)} %get-tuple-element.188, s32[1024]{0:T(1024)S(1)} %pad_clamp_fusion.3), kind=kCustom, calls=%fused_computation.clone.1 | custom fusion | bytes 7340256 | tf_op jit(solution)/shard_map/while/body/eval_jaxpr/gather | solution.py:39
  198.4 6.2 %select_reduce_fusion.5 = (bf16[8,128,128]{2,1,0:T(8,128)(2,1)S(1)}, bf16[8,128,128]{2,1,0:T(8,128)(2,1)S(1)}, bf16[8,128,128]{2,1,0:T(8,128)(2,1)S(1)}, bf16[8,128,128]{2,1,0:T(8,128)(2,1)S(1)}) fusion(pred[8,7,2]{2,1,0:T(8,128)(4,1)S(1)} %copy.77, pred[8,7,2]{2,1,0:T(8,128)(4,1)S(1)} %copy.78, pred[8,7,2]{2,1,0:T(8,128)(4,1)S(1)} %copy.79, ...), kind=kOutput, calls=%fused_computation.5.clone.1 | convolution fusion | flops 483917824 | bytes 6554052 | tf_op jit(solution)/shard_map/while/body/eval_jaxpr/rkab,rklbc->rklac/dot_general | solution.py:40
  204.7 3.1 convert_bitcast_fusion.6
  207.7 3.0 copy.82
  213.2 5.8 %gather_fusion = bf16[56,2,128,128]{3,2,1,0:T(8,128)(2,1)} fusion(bf16[104,2,128,128]{3,2,1,0:T(8,128)(2,1)} %get-tuple-element.188, s32[1024]{0:T(1024)S(1)} %pad_clamp_fusion.3), kind=kCustom, calls=%fused_computation.clone.1 | custom fusion | bytes 7340256 | tf_op jit(solution)/shard_map/while/body/eval_jaxpr/gather | solution.py:39
  219.0 6.2 %select_reduce_fusion.5 = (bf16[8,128,128]{2,1,0:T(8,128)(2,1)S(1)}, bf16[8,128,128]{2,1,0:T(8,128)(2,1)S(1)}, bf16[8,128,128]{2,1,0:T(8,128)(2,1)S(1)}, bf16[8,128,128]{2,1,0:T(8,128)(2,1)S(1)}) fusion(pred[8,7,2]{2,1,0:T(8,128)(4,1)S(1)} %copy.77, pred[8,7,2]{2,1,0:T(8,128)(4,1)S(1)} %copy.78, pred[8,7,2]{2,1,0:T(8,128)(4,1)S(1)} %copy.79, ...), kind=kOutput, calls=%fused_computation.5.clone.1 | convolution fusion | flops 483917824 | bytes 6554052 | tf_op jit(solution)/shard_map/while/body/eval_jaxpr/rkab,rklbc->rklac/dot_general | solution.py:40
  225.3 3.1 convert_bitcast_fusion.6
  228.3 3.0 copy.82
  232.9 22.6 %reshape.384 = bf16[144,65536]{1,0:T(8,128)(2,1)} reshape(bf16[9,8,2,4,128,128]{5,4,3,2,1,0:T(8,128)(2,1)} %get-tuple-element.42) | data formatting | bytes 37748736 | tf_op jit(solution)/shard_map/reshape | solution.py:61
  255.4 9.2 %convolution_convert_fusion.1 = bf16[9,65536]{1,0:T(8,128)(2,1)S(1)} fusion(pred[9,144]{0,1:T(8,128)(4,1)S(1)} %and.157, bf16[144,65536]{1,0:T(8,128)(2,1)} %reshape.384), kind=kOutput, calls=%fused_computation.35 | convolution fusion | flops 170459136 | bytes 20055312 | tf_op jit(solution)/shard_map/dot_general | solution.py:87
  265.1 4.5 %collective-permute-start.5 = (bf16[9,4,128,128]{3,2,1,0:T(8,128)(2,1)S(1)}, bf16[9,4,128,128]{3,2,1,0:T(8,128)(2,1)S(1)}, u32[]{:S(2)}, u32[]{:S(2)}) collective-permute-start(bf16[9,4,128,128]{3,2,1,0:T(8,128)(2,1)S(1)} %bitcast.161), channel_id=1, source_target_pairs={{0,4},{4,8},{8,12},{12,16},{16,20},{20,24},{24,28},{1,5},{5,9},{9,... | collective-permute-start | bytes 3538952 | tf_op jit(solution)/shard_map/ppermute | solution.py:15
  275.1 19.7 %fusion.14 = f32[64,16384]{1,0:T(8,128)S(1)} fusion(bf16[72,8,128,128]{3,2,1,0:T(8,128)(2,1)} %bitcast.150, s32[576]{0:T(1024)S(1)} %eq.172), kind=kOutput, calls=%fused_computation.36 | convolution fusion | flops 1207996416 | bytes 23070976 | tf_op jit(solution)/shard_map/dot_general | solution.py:75
  294.8 23.7 %collective-permute-done.5 = bf16[9,4,128,128]{3,2,1,0:T(8,128)(2,1)S(1)} collective-permute-done((bf16[9,4,128,128]{3,2,1,0:T(8,128)(2,1)S(1)}, bf16[9,4,128,128]{3,2,1,0:T(8,128)(2,1)S(1)}, u32[]{:S(2)}, u32[]{:S(2)}) %collective-permute-start.5) | collective-permute-done | bytes 1179680 | tf_op jit(solution)/shard_map/ppermute | solution.py:15
  (170 shorter events, 46.7 us)
Async XLA Ops:
  0.8 13.7 %copy-start.3 = (s32[72,2]{0,1:T(2,128)S(1)}, s32[72,2]{0,1:T(2,128)}, u32[]{:S(2)}) copy-start(s32[72,2]{0,1:T(2,128)} %param.13) | copy-start | bytes 1732
  0.8 14.0 %copy-start.2 = (s32[72,2,4]{0,2,1:T(4,128)S(1)}, s32[72,2,4]{0,2,1:T(4,128)}, u32[]{:S(2)}) copy-start(s32[72,2,4]{0,2,1:T(4,128)} %param.14) | copy-start | bytes 6916
  0.8 18.6 %copy-start.1 = (s32[72,7,2]{0,2,1:T(2,128)S(1)}, s32[72,7,2]{0,2,1:T(2,128)}, u32[]{:S(2)}) copy-start(s32[72,7,2]{0,2,1:T(2,128)} %param.11) | copy-start | bytes 12100
  0.8 18.7 %copy-start.4 = (s32[72,7]{0,1:T(8,128)S(1)}, s32[72,7]{0,1:T(8,128)}, u32[]{:S(2)}) copy-start(s32[72,7]{0,1:T(8,128)} %param.10) | copy-start | bytes 6052
  5.3 36.2 %collective-permute-start.3 = (bf16[8,2,128,128]{3,2,1,0:T(8,128)(2,1)}, bf16[8,2,128,128]{3,2,1,0:T(8,128)(2,1)S(1)}, u32[]{:S(2)}, u32[]{:S(2)}) collective-permute-start(bf16[8,2,128,128]{3,2,1,0:T(8,128)(2,1)} %get-tuple-element.97), channel_id=1, source_target_pairs={{1,0},{2,1},{3,2},{5,4},{6,5},{7,6},{9,8},{10,9},{11,10},{13,12},{... | collective-permute-start | bytes 1572872 | tf_op jit(solution)/shard_map/ppermute | solution.py:15
  7.9 33.6 %collective-permute-start.2 = (bf16[8,2,128,128]{3,2,1,0:T(8,128)(2,1)}, bf16[8,2,128,128]{3,2,1,0:T(8,128)(2,1)S(1)}, u32[]{:S(2)}, u32[]{:S(2)}) collective-permute-start(bf16[8,2,128,128]{3,2,1,0:T(8,128)(2,1)} %get-tuple-element.95), channel_id=1, source_target_pairs={{0,1},{1,2},{2,3},{4,5},{5,6},{6,7},{8,9},{9,10},{10,11},{12,13},{... | collective-permute-start | bytes 1572872 | tf_op jit(solution)/shard_map/ppermute | solution.py:15
  9.2 32.3 %collective-permute-start.1 = (bf16[8,2,128,128]{3,2,1,0:T(8,128)(2,1)S(1)}, bf16[8,2,128,128]{3,2,1,0:T(8,128)(2,1)S(1)}, u32[]{:S(2)}, u32[]{:S(2)}) collective-permute-start(bf16[8,2,128,128]{3,2,1,0:T(8,128)(2,1)S(1)} %get-tuple-element.96), channel_id=1, source_target_pairs={{4,0},{8,4},{12,8},{16,12},{20,16},{24,20},{28,24},{5,1},{9,5},{13... | collective-permute-start | bytes 1572872 | tf_op jit(solution)/shard_map/ppermute | solution.py:15
  12.2 29.3 %collective-permute-start = (bf16[8,2,128,128]{3,2,1,0:T(8,128)(2,1)S(1)}, bf16[8,2,128,128]{3,2,1,0:T(8,128)(2,1)S(1)}, u32[]{:S(2)}, u32[]{:S(2)}) collective-permute-start(bf16[8,2,128,128]{3,2,1,0:T(8,128)(2,1)S(1)} %get-tuple-element.94), channel_id=1, source_target_pairs={{0,4},{4,8},{8,12},{12,16},{16,20},{20,24},{24,28},{1,5},{5,9},{9,... | collective-permute-start | bytes 1572872 | tf_op jit(solution)/shard_map/ppermute | solution.py:15
  15.4 20.9 %collective-permute-start.4 = (s32[9,4]{1,0:T(8,128)S(1)}, s32[9,4]{1,0:T(8,128)S(1)}, u32[]{:S(2)}, u32[]{:S(2)}) collective-permute-start(s32[9,4]{1,0:T(8,128)S(1)} %broadcast_select_fusion.1), channel_id=1, source_target_pairs={{0,4},{4,8},{8,12},{12,16},{16,20},{20,24},{24,28},{1,5},{5,9},{9,... | collective-permute-start | bytes 440 | tf_op jit(solution)/shard_map/ppermute | solution.py:15
  36.3 5.1 %collective-permute-start.6 = (s32[9,4]{1,0:T(8,128)S(1)}, s32[9,4]{1,0:T(8,128)S(1)}, u32[]{:S(2)}, u32[]{:S(2)}) collective-permute-start(s32[9,4]{1,0:T(8,128)S(1)} %broadcast_select_fusion), channel_id=1, source_target_pairs={{4,0},{8,4},{12,8},{16,12},{20,16},{24,20},{28,24},{5,1},{9,5},{13... | collective-permute-start | bytes 440 | tf_op jit(solution)/shard_map/ppermute | solution.py:15
  255.4 14.2 %copy-start = (bf16[144,65536]{1,0:T(8,128)(2,1)S(1)}, bf16[144,65536]{1,0:T(8,128)(2,1)}, u32[]{:S(2)}) copy-start(bf16[144,65536]{1,0:T(8,128)(2,1)} %reshape.384) | copy-start | bytes 56623108
  265.1 53.4 %collective-permute-start.5 = (bf16[9,4,128,128]{3,2,1,0:T(8,128)(2,1)S(1)}, bf16[9,4,128,128]{3,2,1,0:T(8,128)(2,1)S(1)}, u32[]{:S(2)}, u32[]{:S(2)}) collective-permute-start(bf16[9,4,128,128]{3,2,1,0:T(8,128)(2,1)S(1)} %bitcast.161), channel_id=1, source_target_pairs={{0,4},{4,8},{8,12},{12,16},{16,20},{20,24},{24,28},{1,5},{5,9},{9,... | collective-permute-start | bytes 3538952 | tf_op jit(solution)/shard_map/ppermute | solution.py:15
  273.0 48.4 %collective-permute-start.7 = (bf16[9,4,128,128]{3,2,1,0:T(8,128)(2,1)S(1)}, bf16[9,4,128,128]{3,2,1,0:T(8,128)(2,1)S(1)}, u32[]{:S(2)}, u32[]{:S(2)}) collective-permute-start(bf16[9,4,128,128]{3,2,1,0:T(8,128)(2,1)S(1)} %bitcast.162), channel_id=1, source_target_pairs={{4,0},{8,4},{12,8},{16,12},{20,16},{24,20},{28,24},{5,1},{9,5},{13... | collective-permute-start | bytes 3538952 | tf_op jit(solution)/shard_map/ppermute | solution.py:15
where the time goes:
time: 332 us; the launch traced here: 327 us
  local copies, waits for them, and re-layouts  135 us (41%)
  matrix products  117 us (35%)
  waiting for transfers between devices  42.4 us (13%)
  starting transfers between devices  23.8 us (7%)
  other arithmetic  7.99 us (2%)
    dot_general x9, matrix products, one_block(): jnp.einsum('rkab,rklbc->rklac', a_part, gathered, preferred_element_type=...  56.2 us
    gather x9, local copies, waits for them, and re-layouts, one_block(): gathered = buffer[col_part]  52.6 us
    ppermute x8, waiting for transfers between devices, passed_along(): return lax.ppermute(block, axis, route)  42.4 us
    dynamic_update_slice x18, local copies, waits for them, and re-layouts, local(): lax.map(one_block, (a_tiles.reshape((block_count, block_rows) + a_tiles.s...  40.6 us
    dot_general x9, matrix products, one_block(): jnp.einsum('rjba,rsbc->rjsac', p_part, strip, preferred_element_type=jnp....  27.6 us
    ppermute x8, starting transfers between devices, passed_along(): return lax.ppermute(block, axis, route)  23.8 us
    reshape x1, local copies, waits for them, and re-layouts, local(): by_tile_row = folded.reshape(rows_here * 2, slot_count * tile_area)  22.6 us
    dot_general x1, matrix products, local(): jnp.dot(local_select, by_tile_row.reshape(rows_here * 2 * slot_count, til...  19.7 us
  transfers between devices with their start and end apart: 8, of which 4 were waited for; matrix products, arithmetic and copies ran while one was open for 8% of the time, Pallas kernels for 0%

commit v1 on v0

v1 whole, which is shorter than its diff:
```python
import math

import jax
import jax.numpy as jnp
from jax import lax
from jax.experimental import pallas as pl
from jax.experimental.pallas import tpu as pltpu
from jax.sharding import PartitionSpec as P

COARSE_SLOTS = 16
CR_DEV = 4
SMEM = pltpu.SMEM
VMEM = pltpu.VMEM
ANY = pl.ANY
VMEM_LIMIT = 56 * 1024 * 1024

COLS, SLOTS, AGG, MOVE, ZS = 0, 7, 21, 23, 24


def passed_along(block, axis, distance):
    devices = range(lax.axis_size(axis))
    route = [(i - distance, i) for i in devices if i - distance in devices]
    return lax.ppermute(block, axis, route)


def pick_kernel(capacity, table, send, p_ref, *refs):
    outs, (rows_out, up_out, down_out), sems = refs[:4], refs[4:7], refs[7]
    sends = send.shape[2]
    copies = []
    for q in range(4):
        for j in range(sends):
            copies.append(
                pltpu.make_async_copy(
                    p_ref.at[send[0, q, j]], outs[q].at[j], sems.at[q * sends + j]
                )
            )
    for c in copies:
        c.start()
    for m in range(2 * capacity):
        rows_out[m] = 0
    for m in range(capacity):
        for s in range(4):
            up_out[m, s] = -1
            down_out[m, s] = -1

    def step(i, counts):
        n_up, n_down = counts
        move = table[i, MOVE]

        @pl.when(move == 1)
        def _():
            rows_out[n_up] = i
            for s in range(4):
                up_out[n_up, s] = table[i, AGG + 1] * COARSE_SLOTS + table[i, ZS + 4 + s]

        @pl.when(move == -1)
        def _():
            rows_out[capacity + n_down] = i
            for s in range(4):
                down_out[n_down, s] = table[i, AGG + 1] * COARSE_SLOTS + table[i, ZS + 4 + s]

        return (
            n_up + (move == 1).astype(jnp.int32),
            n_down + (move == -1).astype(jnp.int32),
        )

    lax.fori_loop(0, table.shape[0], step, (jnp.int32(0), jnp.int32(0)))
    for c in copies:
        c.wait()


def load_all(p_ref, ghosts, pall, sems):
    rows_here = p_ref.shape[0]
    sends = ghosts[0].shape[0]
    copies = [pltpu.make_async_copy(p_ref, pall.at[pl.ds(0, rows_here)], sems.at[0])]
    for q in range(4):
        copies.append(
            pltpu.make_async_copy(
                ghosts[q], pall.at[pl.ds(rows_here + q * sends, sends)], sems.at[1 + q]
            )
        )
    return copies


def strips_of(a_row, table, i, pall, acc):
    acc[...] = jnp.zeros_like(acc)
    for k in range(7):
        v = table[i, COLS + k]
        wide = jnp.concatenate([pall[v, 0], pall[v, 1]], axis=1)
        product = jnp.dot(a_row[k], wide, preferred_element_type=jnp.float32)
        for l in range(2):
            s = table[i, SLOTS + 2 * k + l]
            acc[s] += product[:, 128 * l : 128 * (l + 1)]
    return jnp.concatenate([acc[s].astype(jnp.bfloat16) for s in range(4)], axis=1)


def fold(left, strip):
    return lax.dot_general(
        left, strip, (((0,), (0,)), ((), ())), preferred_element_type=jnp.float32
    )


def outbox_kernel(capacity, table, rows, a_ref, p_ref, g0, g1, g2, g3, up, down, pall, abuf, acc, sems):
    copies = load_all(p_ref, (g0, g1, g2, g3), pall, sems)
    for c in copies:
        c.start()
    arows = [
        pltpu.make_async_copy(a_ref.at[rows[m]], abuf.at[m], sems.at[5 + m])
        for m in range(2 * capacity)
    ]
    for c in arows:
        c.start()
    for c in copies + arows:
        c.wait()
    for side, out in enumerate((up, down)):

        def step(m, carry, side=side, out=out):
            i = rows[side * capacity + m]
            strip = strips_of(abuf.at[side * capacity + m], table, i, pall, acc)
            part = fold(pall[i, 1], strip)
            for s in range(4):
                out[m, s] = part[:, 128 * s : 128 * (s + 1)].astype(jnp.bfloat16)
            return carry

        lax.fori_loop(0, capacity, step, 0)


def main_kernel(table, a_ref, p_ref, g0, g1, g2, g3, out, pall, acc, sems):
    g = pl.program_id(0)
    block = a_ref.shape[0]

    @pl.when(g == 0)
    def _():
        copies = load_all(p_ref, (g0, g1, g2, g3), pall, sems)
        for c in copies:
            c.start()
        out[...] = jnp.zeros_like(out)
        for c in copies:
            c.wait()

    def step(b, carry):
        i = g * block + b
        strip = strips_of(a_ref.at[b], table, i, pall, acc)
        part = fold(pall[i, 0], strip)
        base = table[i, AGG] * COARSE_SLOTS
        for s in range(4):
            out[base + table[i, ZS + s]] += part[:, 128 * s : 128 * (s + 1)]

        @pl.when(table[i, MOVE] == 0)
        def _():
            part = fold(pall[i, 1], strip)
            base = table[i, AGG + 1] * COARSE_SLOTS
            for s in range(4):
                out[base + table[i, ZS + 4 + s]] += part[:, 128 * s : 128 * (s + 1)]

        return carry

    lax.fori_loop(0, block, step, 0)


def add_kernel(up_tags, down_tags, up, down, c_in, c_out):
    g = pl.program_id(0)
    c_out[...] = c_in[...]
    for tags, got in ((up_tags, up), (down_tags, down)):

        def step(m, carry, tags=tags, got=got):
            for s in range(4):
                t = tags[m, s]

                @pl.when((t >= 0) & (t // COARSE_SLOTS == g))
                def _():
                    c_out[0, t % COARSE_SLOTS] += got[m, s].astype(jnp.float32)

            return carry

        lax.fori_loop(0, got.shape[0], step, 0)


def local(a_tiles, a_cols, ap_slot, p_tiles, p_aggs, z_slot, send_rows):
    rows_here, _, tile, _ = a_tiles.shape
    sends = send_rows.shape[2]
    capacity = max(2, rows_here // 8)
    col_devices = lax.axis_size("cols")
    row_index = lax.axis_index("rows")
    move = p_aggs[:, 1:] // CR_DEV // col_devices - row_index
    table = jnp.concatenate(
        [
            a_cols,
            ap_slot.reshape(rows_here, 14),
            p_aggs % CR_DEV,
            move,
            z_slot.reshape(rows_here, 8),
        ],
        axis=1,
    )
    smem = pl.BlockSpec(memory_space=SMEM)
    anys = pl.BlockSpec(memory_space=ANY)
    vmem = pl.BlockSpec(memory_space=VMEM)
    ghost = jax.ShapeDtypeStruct((sends, 2, tile, tile), jnp.bfloat16)
    tags = jax.ShapeDtypeStruct((capacity, 4), jnp.int32)
    *sending, rows, up_tags, down_tags = pl.pallas_call(
        lambda *r: pick_kernel(capacity, *r),
        out_shape=[ghost] * 4 + [jax.ShapeDtypeStruct((2 * capacity,), jnp.int32), tags, tags],
        in_specs=[smem, smem, anys],
        out_specs=[anys] * 4 + [smem] * 3,
        scratch_shapes=[pltpu.SemaphoreType.DMA((4 * sends,))],
    )(table, send_rows, p_tiles)
    ghosts = [
        passed_along(sending[0], "rows", 1),
        passed_along(sending[1], "rows", -1),
        passed_along(sending[2], "cols", 1),
        passed_along(sending[3], "cols", -1),
    ]
    up_tags = passed_along(up_tags + 1, "rows", 1) - 1
    down_tags = passed_along(down_tags + 1, "rows", -1) - 1
    box = jax.ShapeDtypeStruct((capacity, 4, tile, tile), jnp.bfloat16)
    all_rows = rows_here + 4 * sends
    params = pltpu.CompilerParams(vmem_limit_bytes=VMEM_LIMIT)
    up, down = pl.pallas_call(
        lambda *r: outbox_kernel(capacity, *r),
        out_shape=[box, box],
        in_specs=[smem, smem] + [anys] * 6,
        out_specs=[vmem, vmem],
        scratch_shapes=[
            VMEM((all_rows, 2, tile, tile), jnp.bfloat16),
            VMEM((2 * capacity, 7, tile, tile), jnp.bfloat16),
            VMEM((4, tile, tile), jnp.float32),
            pltpu.SemaphoreType.DMA((5 + 2 * capacity,)),
        ],
        compiler_params=params,
    )(table, rows, a_tiles, p_tiles, *ghosts)
    up = passed_along(up, "rows", 1)
    down = passed_along(down, "rows", -1)
    block = math.gcd(rows_here, 8)
    tile_count = CR_DEV * COARSE_SLOTS
    coarse = pl.pallas_call(
        main_kernel,
        out_shape=jax.ShapeDtypeStruct((tile_count, tile, tile), jnp.float32),
        grid=(rows_here // block,),
        in_specs=[
            smem,
            pl.BlockSpec((block, 7, tile, tile), lambda g: (g, 0, 0, 0)),
        ]
        + [anys] * 5,
        out_specs=pl.BlockSpec((tile_count, tile, tile), lambda g: (0, 0, 0)),
        scratch_shapes=[
            VMEM((all_rows, 2, tile, tile), jnp.bfloat16),
            VMEM((4, tile, tile), jnp.float32),
            pltpu.SemaphoreType.DMA((5,)),
        ],
        compiler_params=params,
        cost_estimate=pl.CostEstimate(
            flops=2 * rows_here * 22 * tile**3, bytes_accessed=26_000_000, transcendentals=0
        ),
    )(table, a_tiles, p_tiles, *ghosts)
    coarse = coarse.reshape(CR_DEV, COARSE_SLOTS, tile, tile)
    part = pl.BlockSpec((1, COARSE_SLOTS, tile, tile), lambda g: (g, 0, 0, 0))
    whole = pl.BlockSpec((capacity, 4, tile, tile), lambda g: (0, 0, 0, 0))
    return pl.pallas_call(
        add_kernel,
        out_shape=jax.ShapeDtypeStruct(coarse.shape, jnp.float32),
        grid=(CR_DEV,),
        in_specs=[smem, smem, whole, whole, part],
        out_specs=part,
        compiler_params=params,
    )(up_tags, down_tags, up, down, coarse)


def solution(mesh):
    spec = P(("rows", "cols"))
    return jax.shard_map(
        local,
        mesh=mesh,
        in_specs=(spec,) * 7,
        out_specs=spec,
        check_vma=False,
    )
```

time: 332 us -> 239 us (0.72)
  Pallas kernels: 0 us -> 147 us
  local copies, waits for them, and re-layouts: 135 us -> 5.36 us
  matrix products: 117 us -> 0 us
  waiting for transfers between devices: 42.4 us -> 56.8 us
  other arithmetic: 7.99 us -> 3.28 us
    pallas_call x0 -> x4, Pallas kernels: none -> 147 us  [the longest x1 67 us: local(): pl.pallas_call(lambda *r: pick_kernel(capacity, *r), out_shape=[ghost] *...]
    dot_general x23 -> x0, matrix products: 117 us -> none  [the longest x9 56.2 us: one_block(): jnp.einsum('rkab,rklbc->rklac', a_part, gathered, preferred_element_type=...]
    gather x10 -> x0, local copies, waits for them, and re-layouts: 55.9 us -> none  [the longest x9 52.6 us: one_block(): gathered = buffer[col_part]]
    dynamic_update_slice x18 -> x0, local copies, waits for them, and re-layouts: 40.6 us -> none  [local(): lax.map(one_block, (a_tiles.reshape((block_count, block_rows) + a_tiles.s...]
    reshape x3 -> x1, local copies, waits for them, and re-layouts: 22.7 us -> 0.7 us  [local(): ap_slot.reshape(rows_here, 14)]
    ppermute x8, waiting for transfers between devices: 42.4 us -> 56.8 us  [passed_along(): return lax.ppermute(block, axis, route)]
    concatenate x1 -> x0, other arithmetic: 5.72 us -> none  [local(): jnp.concatenate([p_tiles, arrived.reshape((-1,) + p_tiles.shape[1:])], 0)]
    eq x39 -> x0, local copies, waits for them, and re-layouts: 5.68 us -> none  [the longest x36 5.39 us: one_block(): masked = jnp.where((slot_part == slot_value)[..., None, None], product, 0.0)]
  transfers between devices with their start and end apart: 8 -> 8, of which waited for: 4 -> 3; matrix products, arithmetic and copies ran while one was open for 8% -> 1% of each run, Pallas kernels for 0% -> 30%
where the time goes in v1:
time: 239 us; the launch traced here: 234 us
  Pallas kernels  147 us (62%)
  waiting for transfers between devices  56.8 us (24%)
  starting transfers between devices  21.6 us (9%)
  local copies, waits for them, and re-layouts  5.36 us (2%)
  other arithmetic  3.28 us (1%)
    pallas_call x1, Pallas kernels, local(): pl.pallas_call(lambda *r: pick_kernel(capacity, *r), out_shape=[ghost] *...  67 us
    ppermute x8, waiting for transfers between devices, passed_along(): return lax.ppermute(block, axis, route)  56.8 us
    pallas_call x1, Pallas kernels, local(): pl.pallas_call(main_kernel, out_shape=jax.ShapeDtypeStruct((tile_count, t...  55.9 us
    ppermute x8, starting transfers between devices, passed_along(): return lax.ppermute(block, axis, route)  21.6 us
    pallas_call x1, Pallas kernels, local(): pl.pallas_call(lambda *r: outbox_kernel(capacity, *r), out_shape=[box, bo...  15.4 us
    pallas_call x1, Pallas kernels, local(): pl.pallas_call(add_kernel, out_shape=jax.ShapeDtypeStruct(coarse.shape, j...  8.72 us
  transfers between devices with their start and end apart: 8, of which 3 were waited for; matrix products, arithmetic and copies ran while one was open for 1% of the time, Pallas kernels for 30%

profile of v1, /device:TPU:13, one launch (start us, length us, event | category | flops | bytes accessed | tf_op | source)
XLA Modules:
  0.0 234.3 jit_solution(1220648788235110907)
XLA Ops:
  0.0 0.7 and_select_fusion.2
  0.7 0.7 fusion.1
  1.4 0.7 reshape.9
  2.1 1.4 concatenate.3
  3.5 0.7 copy.26.r_0_.table
  4.2 67.0 %shard_map.73 = (bf16[8,2,128,128]{3,2,1,0:T(8,128)(2,1)}, bf16[8,2,128,128]{3,2,1,0:T(8,128)(2,1)}, bf16[8,2,128,128]{3,2,1,0:T(8,128)(2,1)}, bf16[8,2,128,128]...) custom-call(s32[72,32]{1,0:T(8,128)} %copy.26.r_0_.table, s32[1,4,8]{2,1,0:T(4,128)} %r_1_.1, ...), custom_call_target="tpu_custom_call" | custom-call | tf_op jit(solution)/shard_map/pallas_call | solution.py:201
  71.2 3.1 %collective-permute-start.2 = (bf16[8,2,128,128]{3,2,1,0:T(8,128)(2,1)}, bf16[8,2,128,128]{3,2,1,0:T(8,128)(2,1)S(1)}, u32[]{:S(2)}, u32[]{:S(2)}) collective-permute-start(bf16[8,2,128,128]{3,2,1,0:T(8,128)(2,1)} %get-tuple-element.17), channel_id=1, source_target_pairs={{0,4},{4,8},{8,12},{12,16},{16,20},{20,24},{24,28},{1,5},{5,9},{9,... | collective-permute-start | bytes 1572872 | tf_op jit(solution)/shard_map/ppermute | solution.py:23
  74.4 3.1 %collective-permute-start.3 = (bf16[8,2,128,128]{3,2,1,0:T(8,128)(2,1)}, bf16[8,2,128,128]{3,2,1,0:T(8,128)(2,1)S(1)}, u32[]{:S(2)}, u32[]{:S(2)}) collective-permute-start(bf16[8,2,128,128]{3,2,1,0:T(8,128)(2,1)} %get-tuple-element.18), channel_id=1, source_target_pairs={{4,0},{8,4},{12,8},{16,12},{20,16},{24,20},{28,24},{5,1},{9,5},{13... | collective-permute-start | bytes 1572872 | tf_op jit(solution)/shard_map/ppermute | solution.py:23
  77.4 1.3 collective-permute-start.4
  78.7 3.8 %collective-permute-start.5 = (bf16[8,2,128,128]{3,2,1,0:T(8,128)(2,1)}, bf16[8,2,128,128]{3,2,1,0:T(8,128)(2,1)S(1)}, u32[]{:S(2)}, u32[]{:S(2)}) collective-permute-start(bf16[8,2,128,128]{3,2,1,0:T(8,128)(2,1)} %get-tuple-element.20), channel_id=1, source_target_pairs={{1,0},{2,1},{3,2},{5,4},{6,5},{7,6},{9,8},{10,9},{11,10},{13,12},{... | collective-permute-start | bytes 1572872 | tf_op jit(solution)/shard_map/ppermute | solution.py:23
  82.6 0.7 broadcast_add_fusion.2
  83.3 2.1 collective-permute-start.1
  85.4 11.3 %collective-permute-done.2.r_4_.g0 = bf16[8,2,128,128]{3,2,1,0:T(8,128)(2,1)S(1)} collective-permute-done((bf16[8,2,128,128]{3,2,1,0:T(8,128)(2,1)}, bf16[8,2,128,128]{3,2,1,0:T(8,128)(2,1)S(1)}, u32[]{:S(2)}, u32[]{:S(2)}) %collective-permute-start.2) | collective-permute-done | bytes 524320 | tf_op jit(solution)/shard_map/ppermute | solution.py:23
  96.7 0.0 copy-start
  96.7 2.7 %collective-permute-done.3.r_5_.g1 = bf16[8,2,128,128]{3,2,1,0:T(8,128)(2,1)S(1)} collective-permute-done((bf16[8,2,128,128]{3,2,1,0:T(8,128)(2,1)}, bf16[8,2,128,128]{3,2,1,0:T(8,128)(2,1)S(1)}, u32[]{:S(2)}, u32[]{:S(2)}) %collective-permute-start.3) | collective-permute-done | bytes 524320 | tf_op jit(solution)/shard_map/ppermute | solution.py:23
  99.3 0.0 copy-start.1
  99.3 0.0 collective-permute-done.4.r_6_.g2
  99.3 0.0 copy-start.2
  99.3 0.0 collective-permute-done.5.r_7_.g3
  99.3 0.0 copy-start.3
  99.4 0.0 copy-done
  99.4 0.8 copy-done.1
  100.2 0.2 copy-done.2
  100.3 0.2 copy-done.3
  100.5 0.0 copy-start.6
  100.5 15.4 %shard_map.74 = (bf16[9,4,128,128]{3,2,1,0:T(8,128)(2,1)}, bf16[9,4,128,128]{3,2,1,0:T(8,128)(2,1)}) custom-call(s32[72,32]{1,0:T(8,128)} %copy.26.r_0_.table, s32[18]{0:T(128)} %get-tuple-element.16.r_1_, bf16[72,7,128,128]{3,2,1,0:T(8,128)(2,1)} %a_ref.1, bf16[72,2,128,128]{3,2,1,0:T(8,128)(2,1)} %p_ref.1, bf16[8,2,128,128]{3,2,1,0:T(8,128)(2,1)} %copy-done, ...), custom_call_target="tpu_custom_call" | custom-call | tf_op jit(solution)/shard_map/pallas_call | solution.py:219
  115.9 1.9 collective-permute-start.6
  117.9 4.3 %collective-permute-start.7 = (bf16[9,4,128,128]{3,2,1,0:T(8,128)(2,1)}, bf16[9,4,128,128]{3,2,1,0:T(8,128)(2,1)S(1)}, u32[]{:S(2)}, u32[]{:S(2)}) collective-permute-start(bf16[9,4,128,128]{3,2,1,0:T(8,128)(2,1)} %get-tuple-element.22), channel_id=1, source_target_pairs={{4,0},{8,4},{12,8},{16,12},{20,16},{24,20},{28,24},{5,1},{9,5},{13... | collective-permute-start | bytes 3538952 | tf_op jit(solution)/shard_map/ppermute | solution.py:23
  122.1 0.0 copy-done.6
  122.1 2.0 collective-permute-start
  124.2 0.0 collective-permute-done.1
  124.2 0.6 broadcast_add_fusion.down_tags
  124.8 42.8 %collective-permute-done = s32[9,4]{1,0:T(8,128)S(1)} collective-permute-done((s32[9,4]{1,0:T(8,128)S(1)}, s32[9,4]{1,0:T(8,128)S(1)}, u32[]{:S(2)}, u32[]{:S(2)}) %collective-permute-start) | collective-permute-done | bytes 176 | tf_op jit(solution)/shard_map/ppermute | solution.py:23
  167.6 0.6 broadcast_add_fusion.1.up_tags
  168.2 55.9 %shard_map.75 = f32[64,128,128]{2,1,0:T(8,128)} custom-call(s32[72,32]{1,0:T(8,128)} %copy.26.r_0_.table, bf16[72,7,128,128]{3,2,1,0:T(8,128)(2,1)} %a_ref.1, bf16[72,2,128,128]{3,2,1,0:T(8,128)(2,1)} %p_ref.1, bf16[8,2,128,128]{3,2,1,0:T(8,128)(2,1)} %copy-done, bf16[8,2,128,128]{3,2,1,0:T(8,128)(2,1)} %copy-done.1, bf16[8,2,128,128]{3,2,1,0:T(8,128)(2,1)} %copy-done.2, ...), custom_call_target="tpu_custom_call" | custom-call | flops 6643777536 | bytes 26000000 | tf_op jit(solution)/shard_map/pallas_call | solution.py:236
  224.1 0.0 collective-permute-done.6.up
  224.1 0.0 copy-start.4
  224.1 0.0 collective-permute-done.7.down
  224.2 0.0 copy-start.5
  224.2 1.0 copy-done.4
  225.2 0.3 copy-done.5
  225.5 8.7 %shard_map.76 = f32[4,16,128,128]{3,2,1,0:T(8,128)} custom-call(s32[9,4]{1,0:T(8,128)} %broadcast_add_fusion.1.up_tags, s32[9,4]{1,0:T(8,128)} %broadcast_add_fusion.down_tags, bf16[9,4,128,128]{3,2,1,0:T(8,128)(2,1)} %copy-done.4, bf16[9,4,128,128]{3,2,1,0:T(8,128)(2,1)} %copy-done.5, f32[4,16,128,128]{3,2,1,0:T(8,128)} %bitcast.4), custom_call_target="tpu_custom_call" | custom-call | tf_op jit(solution)/shard_map/pallas_call | solution.py:259
  (1 shorter events, 0.0 us)
Async XLA Ops:
  71.2 25.4 %collective-permute-start.2 = (bf16[8,2,128,128]{3,2,1,0:T(8,128)(2,1)}, bf16[8,2,128,128]{3,2,1,0:T(8,128)(2,1)S(1)}, u32[]{:S(2)}, u32[]{:S(2)}) collective-permute-start(bf16[8,2,128,128]{3,2,1,0:T(8,128)(2,1)} %get-tuple-element.17), channel_id=1, source_target_pairs={{0,4},{4,8},{8,12},{12,16},{16,20},{20,24},{24,28},{1,5},{5,9},{9,... | collective-permute-start | bytes 1572872 | tf_op jit(solution)/shard_map/ppermute | solution.py:23
  74.4 25.0 %collective-permute-start.3 = (bf16[8,2,128,128]{3,2,1,0:T(8,128)(2,1)}, bf16[8,2,128,128]{3,2,1,0:T(8,128)(2,1)S(1)}, u32[]{:S(2)}, u32[]{:S(2)}) collective-permute-start(bf16[8,2,128,128]{3,2,1,0:T(8,128)(2,1)} %get-tuple-element.18), channel_id=1, source_target_pairs={{4,0},{8,4},{12,8},{16,12},{20,16},{24,20},{28,24},{5,1},{9,5},{13... | collective-permute-start | bytes 1572872 | tf_op jit(solution)/shard_map/ppermute | solution.py:23
  77.4 21.9 %collective-permute-start.4 = (bf16[8,2,128,128]{3,2,1,0:T(8,128)(2,1)}, bf16[8,2,128,128]{3,2,1,0:T(8,128)(2,1)S(1)}, u32[]{:S(2)}, u32[]{:S(2)}) collective-permute-start(bf16[8,2,128,128]{3,2,1,0:T(8,128)(2,1)} %get-tuple-element.19), channel_id=1, source_target_pairs={{0,1},{1,2},{2,3},{4,5},{5,6},{6,7},{8,9},{9,10},{10,11},{12,13},{... | collective-permute-start | bytes 1572872 | tf_op jit(solution)/shard_map/ppermute | solution.py:23
  78.7 20.6 %collective-permute-start.5 = (bf16[8,2,128,128]{3,2,1,0:T(8,128)(2,1)}, bf16[8,2,128,128]{3,2,1,0:T(8,128)(2,1)S(1)}, u32[]{:S(2)}, u32[]{:S(2)}) collective-permute-start(bf16[8,2,128,128]{3,2,1,0:T(8,128)(2,1)} %get-tuple-element.20), channel_id=1, source_target_pairs={{1,0},{2,1},{3,2},{5,4},{6,5},{7,6},{9,8},{10,9},{11,10},{13,12},{... | collective-permute-start | bytes 1572872 | tf_op jit(solution)/shard_map/ppermute | solution.py:23
  83.3 40.9 %collective-permute-start.1 = (s32[9,4]{1,0:T(8,128)S(1)}, s32[9,4]{1,0:T(8,128)S(1)}, u32[]{:S(2)}, u32[]{:S(2)}) collective-permute-start(s32[9,4]{1,0:T(8,128)S(1)} %broadcast_add_fusion.2), channel_id=1, source_target_pairs={{4,0},{8,4},{12,8},{16,12},{20,16},{24,20},{28,24},{5,1},{9,5},{13... | collective-permute-start | bytes 440 | tf_op jit(solution)/shard_map/ppermute | solution.py:23
  96.7 2.7 %copy-start = (bf16[8,2,128,128]{3,2,1,0:T(8,128)(2,1)}, bf16[8,2,128,128]{3,2,1,0:T(8,128)(2,1)S(1)}, u32[]{:S(2)}) copy-start(bf16[8,2,128,128]{3,2,1,0:T(8,128)(2,1)S(1)} %collective-permute-done.2.r_4_.g0) | copy-start | bytes 1572868
  99.3 0.8 copy-start.1
  99.3 1.0 copy-start.2
  99.3 1.1 copy-start.3
  100.5 21.6 %copy-start.6 = (s32[9,4]{1,0:T(8,128)S(1)}, s32[9,4]{1,0:T(8,128)}, u32[]{:S(2)}) copy-start(s32[9,4]{1,0:T(8,128)} %get-tuple-element.14) | copy-start | bytes 436
  115.9 108.2 %collective-permute-start.6 = (bf16[9,4,128,128]{3,2,1,0:T(8,128)(2,1)}, bf16[9,4,128,128]{3,2,1,0:T(8,128)(2,1)S(1)}, u32[]{:S(2)}, u32[]{:S(2)}) collective-permute-start(bf16[9,4,128,128]{3,2,1,0:T(8,128)(2,1)} %get-tuple-element.21), channel_id=1, source_target_pairs={{0,4},{4,8},{8,12},{12,16},{16,20},{20,24},{24,28},{1,5},{5,9},{9,... | collective-permute-start | bytes 3538952 | tf_op jit(solution)/shard_map/ppermute | solution.py:23
  117.9 106.3 %collective-permute-start.7 = (bf16[9,4,128,128]{3,2,1,0:T(8,128)(2,1)}, bf16[9,4,128,128]{3,2,1,0:T(8,128)(2,1)S(1)}, u32[]{:S(2)}, u32[]{:S(2)}) collective-permute-start(bf16[9,4,128,128]{3,2,1,0:T(8,128)(2,1)} %get-tuple-element.22), channel_id=1, source_target_pairs={{4,0},{8,4},{12,8},{16,12},{20,16},{24,20},{28,24},{5,1},{9,5},{13... | collective-permute-start | bytes 3538952 | tf_op jit(solution)/shard_map/ppermute | solution.py:23
  122.1 45.5 %collective-permute-start = (s32[9,4]{1,0:T(8,128)S(1)}, s32[9,4]{1,0:T(8,128)S(1)}, u32[]{:S(2)}, u32[]{:S(2)}) collective-permute-start(s32[9,4]{1,0:T(8,128)S(1)} %broadcast_add_fusion.3), channel_id=1, source_target_pairs={{0,4},{4,8},{8,12},{12,16},{16,20},{20,24},{24,28},{1,5},{5,9},{9,... | collective-permute-start | bytes 440 | tf_op jit(solution)/shard_map/ppermute | solution.py:23
  224.1 1.1 copy-start.4
  224.2 1.4 copy-start.5

commit v2 on v0

v2 whole, which is shorter than its diff:
```python
import math

import jax
import jax.numpy as jnp
from jax import lax
from jax.experimental import pallas as pl
from jax.experimental.pallas import tpu as pltpu
from jax.sharding import PartitionSpec as P

COARSE_SLOTS = 16
CR_DEV = 4
TILES = CR_DEV * COARSE_SLOTS
SMEM = pltpu.SMEM
VMEM = pltpu.VMEM
ANY = pl.ANY
DMA = pltpu.SemaphoreType.DMA
MESH = pl.DeviceIdType.MESH
VMEM_LIMIT = 56 * 1024 * 1024
EARLY = 2
TOGETHER = 4

COLS, SLOTS, AGG, MOVE, ZS = 0, 7, 21, 23, 24


def passed_along(block, axis, distance):
    devices = range(lax.axis_size(axis))
    route = [(i - distance, i) for i in devices if i - distance in devices]
    return lax.ppermute(block, axis, route)


def directions():
    r, c = lax.axis_index("rows"), lax.axis_index("cols")
    nr, nc = lax.axis_size("rows"), lax.axis_size("cols")
    return [
        ((r + 1, c), r < nr - 1, r > 0),
        ((r - 1, c), r > 0, r < nr - 1),
        ((r, c + 1), c < nc - 1, c > 0),
        ((r, c - 1), c > 0, c < nc - 1),
    ]


def fold(left, strip):
    return lax.dot_general(
        left, strip, (((0,), (0,)), ((), ())), preferred_element_type=jnp.float32
    )


def front_kernel(
    capacity,
    table,
    send,
    a_ref,
    p_ref,
    table_ref,
    ghost_out,
    early_up,
    early_down,
    table_up,
    table_down,
    late_up,
    late_down,
    pall,
    abuf,
    stage,
    land,
    box_up,
    box_down,
    prod,
    rows,
    sems,
    send_sems,
    recv_sems,
):
    rows_here = p_ref.shape[0]
    sends = send.shape[2]
    dirs = directions()
    p_copy = pltpu.make_async_copy(p_ref, pall.at[pl.ds(0, rows_here)], sems.at[0])
    p_copy.start()
    barrier = pltpu.get_barrier_semaphore()
    for target, sending, _ in dirs:

        @pl.when(sending)
        def _(target=target):
            pl.semaphore_signal(barrier, inc=1, device_id=target, device_id_type=MESH)

    p_copy.wait()
    a_copy = pltpu.make_async_copy(a_ref, abuf, sems.at[1])
    a_copy.start()
    for q in range(4):

        def pick(j, carry, q=q):
            stage[q, j] = pall[send[0, q, j]]
            return carry

        lax.fori_loop(0, sends, pick, 0)
    peers = sum(sending.astype(jnp.int32) for _, sending, _ in dirs)
    pl.semaphore_wait(barrier, peers)

    def remote(n, source, place, q):
        return pltpu.make_async_remote_copy(
            src_ref=source,
            dst_ref=place,
            send_sem=send_sems.at[n],
            recv_sem=recv_sems.at[n],
            device_id=dirs[q][0],
            device_id_type=MESH,
        )

    moves = [
        (remote(q, stage.at[q], land.at[pl.ds(q * sends, sends)], q), q) for q in range(4)
    ] + [(remote(4, table_ref, table_up, 0), 0), (remote(5, table_ref, table_down, 1), 1)]

    def start(pairs):
        for copy, q in pairs:

            @pl.when(dirs[q][1])
            def _(copy=copy):
                copy.start()

    def finish(pairs):
        for copy, q in pairs:

            @pl.when(dirs[q][1])
            def _(copy=copy):
                copy.wait_send()

            @pl.when(dirs[q][2])
            def _(copy=copy):
                copy.wait_recv()

    start(moves)

    zero = jnp.int32(0)

    def scan(i, carry):
        n_up, n_down, found = carry
        move = table[i, MOVE]
        is_up, is_down = move == 1, move == -1
        found = tuple(
            jnp.where(
                is_up & (n_up == m) if m < capacity else is_down & (n_down == m - capacity),
                i,
                old,
            )
            for m, old in enumerate(found)
        )
        return n_up + is_up.astype(jnp.int32), n_down + is_down.astype(jnp.int32), found

    _, _, found = lax.fori_loop(0, rows_here, scan, (zero, zero, (zero,) * (2 * capacity)))
    for m, i in enumerate(found):
        rows[m] = i
    a_copy.wait()
    finish(moves)
    ghost_copy = pltpu.make_async_copy(land, ghost_out, sems.at[2])
    ghost_copy.start()
    pall[pl.ds(rows_here, 4 * sends)] = land[...]

    def products(m, places):
        strips = []
        lines = [rows[m], rows[capacity + m]]
        for side, i in enumerate(lines):
            for k in range(7):
                v = table[i, COLS + k]
                wide = jnp.concatenate([pall[v, 0], pall[v, 1]], axis=1)
                prod[side, k] = jnp.dot(abuf[i, k], wide, preferred_element_type=jnp.float32)
        for side, i in enumerate(lines):
            slots = [table[i, SLOTS + n] for n in range(14)]
            gains = [[(x == s).astype(jnp.float32) for s in range(4)] for x in slots]
            chunks = []
            for top in range(0, 128, 16):
                sums = [None] * 4
                for n in range(14):
                    k, l = n // 2, n % 2
                    value = prod[side, k, top : top + 16, 128 * l : 128 * (l + 1)]
                    for s in range(4):
                        term = value * gains[n][s]
                        sums[s] = term if n == 0 else sums[s] + term
                chunks.append(jnp.concatenate([x.astype(jnp.bfloat16) for x in sums], axis=1))
            strips.append(jnp.concatenate(chunks, axis=0))
        for side, i in enumerate(lines):
            part = fold(pall[i, 1], strips[side])
            out, place = places[side]
            for s in range(4):
                out[place, s] = part[:, 128 * s : 128 * (s + 1)].astype(jnp.bfloat16)

    def early_step(m, carry):
        products(m, ((box_up, m), (box_down, m)))
        return carry

    def late_step(m, carry):
        products(m, ((late_up, m - EARLY), (late_down, m - EARLY)))
        return carry

    lax.fori_loop(0, EARLY, early_step, 0)
    early = [(remote(6, box_up, early_up, 0), 0), (remote(7, box_down, early_down, 1), 1)]
    start(early)
    lax.fori_loop(EARLY, capacity, late_step, 0)
    ghost_copy.wait()
    finish(early)


def main_kernel(
    capacity, flags, table, table_up, table_down, a_ref, p_ref, ghosts, early_up, early_down,
    out, tags, pall, got, sems, *accs
):
    g = pl.program_id(0)
    block = a_ref.shape[0]
    rows_here = p_ref.shape[0]

    @pl.when(g == 0)
    def _():
        copies = [
            pltpu.make_async_copy(p_ref, pall.at[pl.ds(0, rows_here)], sems.at[0]),
            pltpu.make_async_copy(ghosts, pall.at[pl.ds(rows_here, ghosts.shape[0])], sems.at[1]),
            pltpu.make_async_copy(early_up, got.at[0], sems.at[2]),
            pltpu.make_async_copy(early_down, got.at[1], sems.at[3]),
        ]
        for c in copies:
            c.start()
        out[...] = jnp.zeros_like(out)
        for m in range(2 * capacity):
            tags[m, 0] = -1
        for side, (other, sign) in enumerate(((table_up, 1), (table_down, -1))):

            @pl.when(flags[side] == 1)
            def _(side=side, other=other, sign=sign):
                def scan(i, n):
                    hit = other[i, MOVE] == sign

                    @pl.when(hit)
                    def _():
                        tags[side * capacity + n, 0] = other[i, AGG + 1]
                        for s in range(4):
                            tags[side * capacity + n, 1 + s] = other[i, ZS + 4 + s]

                    return n + hit.astype(jnp.int32)

                lax.fori_loop(0, rows_here, scan, jnp.int32(0))

        for c in copies:
            c.wait()
        for side in range(2):
            for m in range(EARLY):
                a = tags[side * capacity + m, 0]

                @pl.when(a >= 0)
                def _(side=side, m=m, a=a):
                    for s in range(4):
                        t = a * COARSE_SLOTS + tags[side * capacity + m, 1 + s]
                        out[t] += got[side, m, s].astype(jnp.float32)

    def step(b, carry):
        first = b * TOGETHER
        lines = [g * block + first + n for n in range(TOGETHER)]
        for acc in accs:
            acc[...] = jnp.zeros_like(acc)
        for k in range(7):
            for n, i in enumerate(lines):
                v = table[i, COLS + k]
                wide = jnp.concatenate([pall[v, 0], pall[v, 1]], axis=1)
                product = jnp.dot(a_ref[first + n, k], wide, preferred_element_type=jnp.float32)
                for l in range(2):
                    accs[n][table[i, SLOTS + 2 * k + l]] += product[:, 128 * l : 128 * (l + 1)]
        for n, i in enumerate(lines):
            strip = jnp.concatenate([accs[n][s].astype(jnp.bfloat16) for s in range(4)], axis=1)
            for j in range(2):
                part = fold(pall[i, j], strip)
                base = table[i, AGG + j] * COARSE_SLOTS
                for s in range(4):
                    t = base + table[i, ZS + 4 * j + s]
                    if j:
                        t = jnp.where(table[i, MOVE] == 0, t, TILES)
                    out[t] += part[:, 128 * s : 128 * (s + 1)]
        return carry

    lax.fori_loop(0, block // TOGETHER, step, 0)


def add_kernel(capacity, tags, up, down, c_in, c_out):
    g = pl.program_id(0)
    c_out[0] = c_in[...]
    for side, got in ((0, up), (1, down)):

        def step(m, carry, side=side, got=got):
            line = side * capacity + EARLY + m

            @pl.when(tags[line, 0] == g)
            def _():
                for s in range(4):
                    c_out[0, tags[line, 1 + s]] += got[m, s].astype(jnp.float32)

            return carry

        lax.fori_loop(0, got.shape[0], step, 0)


def local(a_tiles, a_cols, ap_slot, p_tiles, p_aggs, z_slot, send_rows):
    rows_here, _, tile, _ = a_tiles.shape
    sends = send_rows.shape[2]
    capacity = max(2, rows_here // 8)
    late = capacity - EARLY
    col_devices = lax.axis_size("cols")
    row_index = lax.axis_index("rows")
    move = p_aggs[:, 1:] // CR_DEV // col_devices - row_index
    table = jnp.concatenate(
        [
            a_cols,
            ap_slot.reshape(rows_here, 14),
            p_aggs % CR_DEV,
            move,
            z_slot.reshape(rows_here, 8),
        ],
        axis=1,
    )
    flags = jnp.stack([row_index > 0, row_index < lax.axis_size("rows") - 1]).astype(jnp.int32)
    smem = pl.BlockSpec(memory_space=SMEM)
    anys = pl.BlockSpec(memory_space=ANY)
    vmem = pl.BlockSpec(memory_space=VMEM)
    bf16 = jnp.bfloat16
    all_rows = rows_here + 4 * sends

    def boxes(n):
        return jax.ShapeDtypeStruct((n, 4, tile, tile), bf16)

    table_shape = jax.ShapeDtypeStruct(table.shape, jnp.int32)
    ghosts, early_up, early_down, table_up, table_down, late_up, late_down = pl.pallas_call(
        lambda *r: front_kernel(capacity, *r),
        out_shape=[
            jax.ShapeDtypeStruct((4 * sends, 2, tile, tile), bf16),
            boxes(EARLY),
            boxes(EARLY),
            table_shape,
            table_shape,
            boxes(late),
            boxes(late),
        ],
        in_specs=[smem, smem] + [anys] * 3,
        out_specs=[anys] * 5 + [vmem] * 2,
        scratch_shapes=[
            VMEM((all_rows, 2, tile, tile), bf16),
            VMEM((rows_here, 7, tile, tile), bf16),
            VMEM((4, sends, 2, tile, tile), bf16),
            VMEM((4 * sends, 2, tile, tile), bf16),
            VMEM((EARLY, 4, tile, tile), bf16),
            VMEM((EARLY, 4, tile, tile), bf16),
            VMEM((2, 7, tile, 2 * tile), jnp.float32),
            SMEM((2 * capacity,), jnp.int32),
            DMA((3,)),
            DMA((8,)),
            DMA((8,)),
        ],
        compiler_params=pltpu.CompilerParams(
            vmem_limit_bytes=VMEM_LIMIT, collective_id=0, has_side_effects=True
        ),
        cost_estimate=pl.CostEstimate(
            flops=2 * capacity * 36 * tile**3, bytes_accessed=25_000_000, transcendentals=0
        ),
    )(table, send_rows, a_tiles, p_tiles, table)
    up = passed_along(late_up, "rows", 1)
    down = passed_along(late_down, "rows", -1)
    block = math.gcd(rows_here, 8)
    params = pltpu.CompilerParams(vmem_limit_bytes=VMEM_LIMIT)
    coarse, tags = pl.pallas_call(
        lambda *r: main_kernel(capacity, *r),
        out_shape=[
            jax.ShapeDtypeStruct((TILES + 1, tile, tile), jnp.float32),
            jax.ShapeDtypeStruct((2 * capacity, 5), jnp.int32),
        ],
        grid=(rows_here // block,),
        in_specs=[smem] * 4
        + [pl.BlockSpec((block, 7, tile, tile), lambda g: (g, 0, 0, 0))]
        + [anys] * 4,
        out_specs=[pl.BlockSpec((TILES + 1, tile, tile), lambda g: (0, 0, 0)), smem],
        scratch_shapes=[
            VMEM((all_rows, 2, tile, tile), bf16),
            VMEM((2, EARLY, 4, tile, tile), bf16),
            DMA((4,)),
        ]
        + [VMEM((4, tile, tile), jnp.float32)] * TOGETHER,
        compiler_params=params,
        cost_estimate=pl.CostEstimate(
            flops=2 * rows_here * 22 * tile**3, bytes_accessed=26_000_000, transcendentals=0
        ),
    )(flags, table, table_up, table_down, a_tiles, p_tiles, ghosts, early_up, early_down)
    whole = pl.BlockSpec((late, 4, tile, tile), lambda g: (0, 0, 0, 0))
    return pl.pallas_call(
        lambda *r: add_kernel(capacity, *r),
        out_shape=jax.ShapeDtypeStruct((CR_DEV, COARSE_SLOTS, tile, tile), jnp.float32),
        grid=(CR_DEV,),
        in_specs=[
            smem,
            whole,
            whole,
            pl.BlockSpec((COARSE_SLOTS, tile, tile), lambda g: (g, 0, 0)),
        ],
        out_specs=pl.BlockSpec((1, COARSE_SLOTS, tile, tile), lambda g: (g, 0, 0, 0)),
        compiler_params=params,
    )(tags, up, down, coarse)


def solution(mesh):
    spec = P(("rows", "cols"))
    return jax.shard_map(
        local,
        mesh=mesh,
        in_specs=(spec,) * 7,
        out_specs=spec,
        check_vma=False,
    )
```

time: 332 us -> 102 us (0.31); the launches traced: 327 us -> 102 us
  local copies, waits for them, and re-layouts: 135 us -> 3.81 us
  matrix products: 117 us -> 0 us
  Pallas kernels: 0 us -> 79.5 us
  waiting for transfers between devices: 42.4 us -> 9.97 us
  starting transfers between devices: 23.8 us -> 6.18 us
  other arithmetic: 7.99 us -> 2.02 us
    dot_general x23 -> x0, matrix products: 117 us -> none  [the longest x9 56.2 us: one_block(): jnp.einsum('rkab,rklbc->rklac', a_part, gathered, preferred_element_type=...]
    pallas_call x0 -> x3, Pallas kernels: none -> 79.5 us  [the longest x1 45.6 us: local(): pl.pallas_call(lambda *r: front_kernel(capacity, *r), out_shape=[jax.Shap...]
    gather x10 -> x0, local copies, waits for them, and re-layouts: 55.9 us -> none  [the longest x9 52.6 us: one_block(): gathered = buffer[col_part]]
    dynamic_update_slice x18 -> x0, local copies, waits for them, and re-layouts: 40.6 us -> none  [local(): lax.map(one_block, (a_tiles.reshape((block_count, block_rows) + a_tiles.s...]
    ppermute x8 -> x2, waiting for transfers between devices: 42.4 us -> 9.97 us  [passed_along(): return lax.ppermute(block, axis, route)]
    reshape x3 -> x1, local copies, waits for them, and re-layouts: 22.7 us -> 0.7 us  [local(): ap_slot.reshape(rows_here, 14)]
    ppermute x8 -> x2, starting transfers between devices: 23.8 us -> 6.18 us  [passed_along(): return lax.ppermute(block, axis, route)]
    concatenate x1 -> x0, other arithmetic: 5.72 us -> none  [local(): jnp.concatenate([p_tiles, arrived.reshape((-1,) + p_tiles.shape[1:])], 0)]
  transfers between devices with their start and end apart: 8 -> 2, of which waited for: 4 -> 2; matrix products, arithmetic and copies ran while one was open for 8% -> 1% of each run, Pallas kernels for 0% -> 28%
where the time goes in v2:
time: 102 us
  Pallas kernels  79.5 us (78%)
  waiting for transfers between devices  9.97 us (10%)
  starting transfers between devices  6.18 us (6%)
  local copies, waits for them, and re-layouts  3.81 us (4%)
  other arithmetic  2.02 us (2%)
    pallas_call x1, Pallas kernels, local(): pl.pallas_call(lambda *r: front_kernel(capacity, *r), out_shape=[jax.Shap...  45.6 us
    pallas_call x1, Pallas kernels, local(): pl.pallas_call(lambda *r: main_kernel(capacity, *r), out_shape=[jax.Shape...  28.1 us
    ppermute x2, waiting for transfers between devices, passed_along(): return lax.ppermute(block, axis, route)  9.97 us
    ppermute x2, starting transfers between devices, passed_along(): return lax.ppermute(block, axis, route)  6.18 us
    pallas_call x1, Pallas kernels, local(): pl.pallas_call(lambda *r: add_kernel(capacity, *r), out_shape=jax.ShapeDt...  5.81 us
    concatenate x2, local copies, waits for them, and re-layouts, local(): jnp.concatenate([a_cols, ap_slot.reshape(rows_here, 14), p_aggs % CR_DEV,...  2.15 us
  transfers between devices with their start and end apart: 2, of which 2 were waited for; matrix products, arithmetic and copies ran while one was open for 1% of the time, Pallas kernels for 28%

profile of v2, /device:TPU:13, one launch (start us, length us, event | category | flops | bytes accessed | tf_op | source)
XLA Modules:
  0.0 101.6 jit_solution(7944160369247079766)
XLA Ops:
  0.0 0.7 and_select_fusion.2
  0.7 0.7 fusion.1
  1.4 0.7 reshape.6
  2.1 1.4 %concatenate.3 = s32[72,32]{0,1:T(8,128)S(1)} concatenate(s32[72,7]{0,1:T(8,128)} %param.8, s32[72,14]{0,1:T(8,128)S(1)} %reshape.6, s32[72,2]{0,1:T(2,128)S(1)} %and_select_fusion.2, s32[72,1]{0,1:T(1,128)S(1)} %fusion.1, s32[72,8]{0,1:T(8,128)} %bitcast.5), dimensions={1} | concatenate | bytes 18432 | tf_op jit(solution)/shard_map/concatenate | solution.py:305
  3.5 0.7 copy.28.r_0_.r_4_.r_1_
  4.2 45.6 %shard_map.73 = (bf16[32,2,128,128]{3,2,1,0:T(8,128)(2,1)}, bf16[2,4,128,128]{3,2,1,0:T(8,128)(2,1)}, bf16[2,4,128,128]{3,2,1,0:T(8,128)(2,1)}, s32[72,32]{1,0:T...) custom-call(s32[72,32]{1,0:T(8,128)} %copy.28.r_0_.r_4_.r_1_, ...), custom_call_target="tpu_custom_call" | custom-call | flops 1358954496 | bytes 25000000 | tf_op jit(solution)/shard_map/pallas_call | solution.py:326
  49.9 3.5 %collective-permute-start = (bf16[7,4,128,128]{3,2,1,0:T(8,128)(2,1)}, bf16[7,4,128,128]{3,2,1,0:T(8,128)(2,1)S(1)}, u32[]{:S(2)}, u32[]{:S(2)}) collective-permute-start(bf16[7,4,128,128]{3,2,1,0:T(8,128)(2,1)} %get-tuple-element.20), channel_id=1, source_target_pairs={{0,4},{4,8},{8,12},{12,16},{16,20},{20,24},{24,28},{1,5},{5,9},{9,... | collective-permute-start | bytes 2752520 | tf_op jit(solution)/shard_map/ppermute | solution.py:28
  53.3 2.7 %collective-permute-start.1 = (bf16[7,4,128,128]{3,2,1,0:T(8,128)(2,1)}, bf16[7,4,128,128]{3,2,1,0:T(8,128)(2,1)S(1)}, u32[]{:S(2)}, u32[]{:S(2)}) collective-permute-start(bf16[7,4,128,128]{3,2,1,0:T(8,128)(2,1)} %get-tuple-element.21), channel_id=1, source_target_pairs={{4,0},{8,4},{12,8},{16,12},{20,16},{24,20},{28,24},{5,1},{9,5},{13... | collective-permute-start | bytes 2752520 | tf_op jit(solution)/shard_map/ppermute | solution.py:28
  56.1 0.6 add_convert_fusion.r_0_
  56.7 28.1 %shard_map.74 = (f32[65,128,128]{2,1,0:T(8,128)}, s32[18,5]{1,0:T(8,128)}) custom-call(s32[2]{0:T(128)} %add_convert_fusion.r_0_, s32[72,32]{1,0:T(8,128)} %copy.28.r_0_.r_4_.r_1_, s32[72,32]{1,0:T(8,128)} %get-tuple-element.14.r_2_, s32[72,32]{1,0:T(8,128)} %get-tuple-element.15.r_3_, bf16[72,7,128,128]{3,2,1,0:T(8,128)(2,1)} %r_4_.1, ...), custom_call_target="tpu_custom_call" | custom-call | flops 6643777536 | bytes 26000000 | tf_op jit(solution)/shard_map/pallas_call | solution.py:363
  84.8 7.1 %collective-permute-done.r_1_ = bf16[7,4,128,128]{3,2,1,0:T(8,128)(2,1)S(1)} collective-permute-done((bf16[7,4,128,128]{3,2,1,0:T(8,128)(2,1)}, bf16[7,4,128,128]{3,2,1,0:T(8,128)(2,1)S(1)}, u32[]{:S(2)}, u32[]{:S(2)}) %collective-permute-start) | collective-permute-done | bytes 917536 | tf_op jit(solution)/shard_map/ppermute | solution.py:28
  91.9 0.0 copy-start
  91.9 2.9 %collective-permute-done.1.r_2_ = bf16[7,4,128,128]{3,2,1,0:T(8,128)(2,1)S(1)} collective-permute-done((bf16[7,4,128,128]{3,2,1,0:T(8,128)(2,1)}, bf16[7,4,128,128]{3,2,1,0:T(8,128)(2,1)S(1)}, u32[]{:S(2)}, u32[]{:S(2)}) %collective-permute-start.1) | collective-permute-done | bytes 917536 | tf_op jit(solution)/shard_map/ppermute | solution.py:28
  94.8 0.0 copy-start.1
  94.8 0.0 copy-done
  94.8 0.9 copy-done.1
  95.8 5.8 %shard_map.75 = f32[4,16,128,128]{3,2,1,0:T(8,128)} custom-call(s32[18,5]{1,0:T(8,128)} %get-tuple-element.19.r_0_, bf16[7,4,128,128]{3,2,1,0:T(8,128)(2,1)} %copy-done, bf16[7,4,128,128]{3,2,1,0:T(8,128)(2,1)} %copy-done.1, f32[65,128,128]{2,1,0:T(8,128)} %get-tuple-element.22.r_3_), custom_call_target="tpu_custom_call" | custom-call | tf_op jit(solution)/shard_map/pallas_call | solution.py:386
Async XLA Ops:
  49.9 42.1 %collective-permute-start = (bf16[7,4,128,128]{3,2,1,0:T(8,128)(2,1)}, bf16[7,4,128,128]{3,2,1,0:T(8,128)(2,1)S(1)}, u32[]{:S(2)}, u32[]{:S(2)}) collective-permute-start(bf16[7,4,128,128]{3,2,1,0:T(8,128)(2,1)} %get-tuple-element.20), channel_id=1, source_target_pairs={{0,4},{4,8},{8,12},{12,16},{16,20},{20,24},{24,28},{1,5},{5,9},{9,... | collective-permute-start | bytes 2752520 | tf_op jit(solution)/shard_map/ppermute | solution.py:28
  53.3 41.5 %collective-permute-start.1 = (bf16[7,4,128,128]{3,2,1,0:T(8,128)(2,1)}, bf16[7,4,128,128]{3,2,1,0:T(8,128)(2,1)S(1)}, u32[]{:S(2)}, u32[]{:S(2)}) collective-permute-start(bf16[7,4,128,128]{3,2,1,0:T(8,128)(2,1)} %get-tuple-element.21), channel_id=1, source_target_pairs={{4,0},{8,4},{12,8},{16,12},{20,16},{24,20},{28,24},{5,1},{9,5},{13... | collective-permute-start | bytes 2752520 | tf_op jit(solution)/shard_map/ppermute | solution.py:28
  91.9 2.9 %copy-start = (bf16[7,4,128,128]{3,2,1,0:T(8,128)(2,1)}, bf16[7,4,128,128]{3,2,1,0:T(8,128)(2,1)S(1)}, u32[]{:S(2)}) copy-start(bf16[7,4,128,128]{3,2,1,0:T(8,128)(2,1)S(1)} %collective-permute-done.r_1_) | copy-start | bytes 2752516
  94.8 1.0 copy-start.1

commit v3 on v2

--- a/solution.py
+++ b/solution.py
@@ -16,10 +16,10 @@
 DMA = pltpu.SemaphoreType.DMA
 MESH = pl.DeviceIdType.MESH
 VMEM_LIMIT = 56 * 1024 * 1024
-EARLY = 2
+MAIN_LIMIT = 32 * 1024 * 1024
+ADD_LIMIT = 20 * 1024 * 1024
+EARLY = 4
 TOGETHER = 4
-
-COLS, SLOTS, AGG, MOVE, ZS = 0, 7, 21, 23, 24
 
 
 def passed_along(block, axis, distance):
@@ -47,16 +47,21 @@
 
 def front_kernel(
     capacity,
-    table,
+    cols,
+    slot,
+    aggs,
     send,
     a_ref,
     p_ref,
-    table_ref,
+    aggs_ref,
+    z_ref,
     ghost_out,
     early_up,
     early_down,
-    table_up,
-    table_down,
+    aggs_up,
+    aggs_down,
+    z_up,
+    z_down,
     late_up,
     late_down,
     pall,
@@ -86,13 +91,6 @@
     p_copy.wait()
     a_copy = pltpu.make_async_copy(a_ref, abuf, sems.at[1])
     a_copy.start()
-    for q in range(4):
-
-        def pick(j, carry, q=q):
-            stage[q, j] = pall[send[0, q, j]]
-            return carry
-
-        lax.fori_loop(0, sends, pick, 0)
     peers = sum(sending.astype(jnp.int32) for _, sending, _ in dirs)
     pl.semaphore_wait(barrier, peers)
 
@@ -108,7 +106,12 @@
 
     moves = [
         (remote(q, stage.at[q], land.at[pl.ds(q * sends, sends)], q), q) for q in range(4)
-    ] + [(remote(4, table_ref, table_up, 0), 0), (remote(5, table_ref, table_down, 1), 1)]
+    ] + [
+        (remote(4, aggs_ref, aggs_up, 0), 0),
+        (remote(5, aggs_ref, aggs_down, 1), 1),
+        (remote(6, z_ref, z_up, 0), 0),
+        (remote(7, z_ref, z_down, 1), 1),
+    ]
 
     def start(pairs):
         for copy, q in pairs:
@@ -128,13 +131,23 @@
             def _(copy=copy):
                 copy.wait_recv()
 
-    start(moves)
-
+    for q in range(4):
+
+        def pick(j, carry, q=q):
+            stage[q, j] = pall[send[0, q, j]]
+            return carry
+
+        lax.fori_loop(0, sends, pick, 0)
+        start(moves[q : q + 1])
+    start(moves[4:])
+
+    row_index = lax.axis_index("rows")
+    row_span = CR_DEV * lax.axis_size("cols")
     zero = jnp.int32(0)
 
     def scan(i, carry):
         n_up, n_down, found = carry
-        move = table[i, MOVE]
+        move = lax.div(aggs[1, i], row_span) - row_index
         is_up, is_down = move == 1, move == -1
         found = tuple(
             jnp.where(
@@ -160,11 +173,11 @@
         lines = [rows[m], rows[capacity + m]]
         for side, i in enumerate(lines):
             for k in range(7):
-                v = table[i, COLS + k]
+                v = cols[k, i]
                 wide = jnp.concatenate([pall[v, 0], pall[v, 1]], axis=1)
                 prod[side, k] = jnp.dot(abuf[i, k], wide, preferred_element_type=jnp.float32)
         for side, i in enumerate(lines):
-            slots = [table[i, SLOTS + n] for n in range(14)]
+            slots = [slot[n // 2, n % 2, i] for n in range(14)]
             gains = [[(x == s).astype(jnp.float32) for s in range(4)] for x in slots]
             chunks = []
             for top in range(0, 128, 16):
@@ -183,29 +196,40 @@
             for s in range(4):
                 out[place, s] = part[:, 128 * s : 128 * (s + 1)].astype(jnp.bfloat16)
 
+    def early_pairs(m):
+        return [
+            (remote(8 + 2 * m, box_up.at[m], early_up.at[m], 0), 0),
+            (remote(9 + 2 * m, box_down.at[m], early_down.at[m], 1), 1),
+        ]
+
     def early_step(m, carry):
         products(m, ((box_up, m), (box_down, m)))
+        start(early_pairs(m))
         return carry
 
     def late_step(m, carry):
         products(m, ((late_up, m - EARLY), (late_down, m - EARLY)))
         return carry
 
+    def early_end(m, carry):
+        finish(early_pairs(m))
+        return carry
+
     lax.fori_loop(0, EARLY, early_step, 0)
-    early = [(remote(6, box_up, early_up, 0), 0), (remote(7, box_down, early_down, 1), 1)]
-    start(early)
     lax.fori_loop(EARLY, capacity, late_step, 0)
     ghost_copy.wait()
-    finish(early)
+    lax.fori_loop(0, EARLY, early_end, 0)
 
 
 def main_kernel(
-    capacity, flags, table, table_up, table_down, a_ref, p_ref, ghosts, early_up, early_down,
-    out, tags, pall, got, sems, *accs
+    capacity, cols, slot, aggs, z, aggs_up, aggs_down, z_up, z_down, a_ref, p_ref, ghosts,
+    early_up, early_down, out, tags, pall, got, sems, *accs
 ):
     g = pl.program_id(0)
     block = a_ref.shape[0]
     rows_here = p_ref.shape[0]
+    row_index = lax.axis_index("rows")
+    row_span = CR_DEV * lax.axis_size("cols")
 
     @pl.when(g == 0)
     def _():
@@ -220,18 +244,23 @@
         out[...] = jnp.zeros_like(out)
         for m in range(2 * capacity):
             tags[m, 0] = -1
-        for side, (other, sign) in enumerate(((table_up, 1), (table_down, -1))):
-
-            @pl.when(flags[side] == 1)
-            def _(side=side, other=other, sign=sign):
+        received = (
+            (aggs_up, z_up, row_index > 0),
+            (aggs_down, z_down, row_index < lax.axis_size("rows") - 1),
+        )
+        for side, (other, other_z, there) in enumerate(received):
+
+            @pl.when(there)
+            def _(side=side, other=other, other_z=other_z):
                 def scan(i, n):
-                    hit = other[i, MOVE] == sign
+                    a = other[1, i]
+                    hit = lax.div(a, row_span) == row_index
 
                     @pl.when(hit)
                     def _():
-                        tags[side * capacity + n, 0] = other[i, AGG + 1]
+                        tags[side * capacity + n, 0] = lax.rem(a, CR_DEV)
                         for s in range(4):
-                            tags[side * capacity + n, 1 + s] = other[i, ZS + 4 + s]
+                            tags[side * capacity + n, 1 + s] = other_z[1, s, i]
 
                     return n + hit.astype(jnp.int32)
 
@@ -256,20 +285,21 @@
             acc[...] = jnp.zeros_like(acc)
         for k in range(7):
             for n, i in enumerate(lines):
-                v = table[i, COLS + k]
+                v = cols[k, i]
                 wide = jnp.concatenate([pall[v, 0], pall[v, 1]], axis=1)
                 product = jnp.dot(a_ref[first + n, k], wide, preferred_element_type=jnp.float32)
                 for l in range(2):
-                    accs[n][table[i, SLOTS + 2 * k + l]] += product[:, 128 * l : 128 * (l + 1)]
+                    accs[n][slot[k, l, i]] += product[:, 128 * l : 128 * (l + 1)]
         for n, i in enumerate(lines):
             strip = jnp.concatenate([accs[n][s].astype(jnp.bfloat16) for s in range(4)], axis=1)
             for j in range(2):
                 part = fold(pall[i, j], strip)
-                base = table[i, AGG + j] * COARSE_SLOTS
+                base = lax.rem(aggs[j, i], CR_DEV) * COARSE_SLOTS
+                here = lax.div(aggs[j, i], row_span) == row_index
                 for s in range(4):
-                    t = base + table[i, ZS + 4 * j + s]
+                    t = base + z[j, s, i]
                     if j:
-                        t = jnp.where(table[i, MOVE] == 0, t, TILES)
+                        t = jnp.where(here, t, TILES)
                     out[t] += part[:, 128 * s : 128 * (s + 1)]
         return carry
 
@@ -296,23 +326,11 @@
 
 def local(a_tiles, a_cols, ap_slot, p_tiles, p_aggs, z_slot, send_rows):
     rows_here, _, tile, _ = a_tiles.shape
+    a_cols, p_aggs = a_cols.T, p_aggs.T
+    ap_slot, z_slot = ap_slot.transpose(1, 2, 0), z_slot.transpose(1, 2, 0)
     sends = send_rows.shape[2]
     capacity = max(2, rows_here // 8)
     late = capacity - EARLY
-    col_devices = lax.axis_size("cols")
-    row_index = lax.axis_index("rows")
-    move = p_aggs[:, 1:] // CR_DEV // col_devices - row_index
-    table = jnp.concatenate(
-        [
-            a_cols,
-            ap_slot.reshape(rows_here, 14),
-            p_aggs % CR_DEV,
-            move,
-            z_slot.reshape(rows_here, 8),
-        ],
-        axis=1,
-    )
-    flags = jnp.stack([row_index > 0, row_index < lax.axis_size("rows") - 1]).astype(jnp.int32)
     smem = pl.BlockSpec(memory_space=SMEM)
     anys = pl.BlockSpec(memory_space=ANY)
     vmem = pl.BlockSpec(memory_space=VMEM)
@@ -322,20 +340,23 @@
     def boxes(n):
         return jax.ShapeDtypeStruct((n, 4, tile, tile), bf16)
 
-    table_shape = jax.ShapeDtypeStruct(table.shape, jnp.int32)
-    ghosts, early_up, early_down, table_up, table_down, late_up, late_down = pl.pallas_call(
+    aggs_shape = jax.ShapeDtypeStruct(p_aggs.shape, jnp.int32)
+    z_shape = jax.ShapeDtypeStruct(z_slot.shape, jnp.int32)
+    ghosts, early_up, early_down, aggs_up, aggs_down, z_up, z_down, late_up, late_down = pl.pallas_call(
         lambda *r: front_kernel(capacity, *r),
         out_shape=[
             jax.ShapeDtypeStruct((4 * sends, 2, tile, tile), bf16),
             boxes(EARLY),
             boxes(EARLY),
-            table_shape,
-            table_shape,
+            aggs_shape,
+            aggs_shape,
+            z_shape,
+            z_shape,
             boxes(late),
             boxes(late),
         ],
-        in_specs=[smem, smem] + [anys] * 3,
-        out_specs=[anys] * 5 + [vmem] * 2,
+        in_specs=[smem] * 4 + [anys] * 4,
+        out_specs=[anys] * 7 + [vmem] * 2,
         scratch_shapes=[
             VMEM((all_rows, 2, tile, tile), bf16),
             VMEM((rows_here, 7, tile, tile), bf16),
@@ -346,8 +367,8 @@
             VMEM((2, 7, tile, 2 * tile), jnp.float32),
             SMEM((2 * capacity,), jnp.int32),
             DMA((3,)),
-            DMA((8,)),
-            DMA((8,)),
+            DMA((8 + 2 * EARLY,)),
+            DMA((8 + 2 * EARLY,)),
         ],
         compiler_params=pltpu.CompilerParams(
             vmem_limit_bytes=VMEM_LIMIT, collective_id=0, has_side_effects=True
@@ -355,11 +376,10 @@
         cost_estimate=pl.CostEstimate(
             flops=2 * capacity * 36 * tile**3, bytes_accessed=25_000_000, transcendentals=0
         ),
-    )(table, send_rows, a_tiles, p_tiles, table)
+    )(a_cols, ap_slot, p_aggs, send_rows, a_tiles, p_tiles, p_aggs, z_slot)
     up = passed_along(late_up, "rows", 1)
     down = passed_along(late_down, "rows", -1)
     block = math.gcd(rows_here, 8)
-    params = pltpu.CompilerParams(vmem_limit_bytes=VMEM_LIMIT)
     coarse, tags = pl.pallas_call(
         lambda *r: main_kernel(capacity, *r),
         out_shape=[
@@ -367,7 +387,7 @@
             jax.ShapeDtypeStruct((2 * capacity, 5), jnp.int32),
         ],
         grid=(rows_here // block,),
-        in_specs=[smem] * 4
+        in_specs=[smem] * 8
         + [pl.BlockSpec((block, 7, tile, tile), lambda g: (g, 0, 0, 0))]
         + [anys] * 4,
         out_specs=[pl.BlockSpec((TILES + 1, tile, tile), lambda g: (0, 0, 0)), smem],
@@ -377,11 +397,14 @@
             DMA((4,)),
         ]
         + [VMEM((4, tile, tile), jnp.float32)] * TOGETHER,
-        compiler_params=params,
+        compiler_params=pltpu.CompilerParams(vmem_limit_bytes=MAIN_LIMIT),
         cost_estimate=pl.CostEstimate(
             flops=2 * rows_here * 22 * tile**3, bytes_accessed=26_000_000, transcendentals=0
         ),
-    )(flags, table, table_up, table_down, a_tiles, p_tiles, ghosts, early_up, early_down)
+    )(
+        a_cols, ap_slot, p_aggs, z_slot, aggs_up, aggs_down, z_up, z_down,
+        a_tiles, p_tiles, ghosts, early_up, early_down,
+    )
     whole = pl.BlockSpec((late, 4, tile, tile), lambda g: (0, 0, 0, 0))
     return pl.pallas_call(
         lambda *r: add_kernel(capacity, *r),
@@ -394,7 +417,7 @@
             pl.BlockSpec((COARSE_SLOTS, tile, tile), lambda g: (g, 0, 0)),
         ],
         out_specs=pl.BlockSpec((1, COARSE_SLOTS, tile, tile), lambda g: (g, 0, 0, 0)),
-        compiler_params=params,
+        compiler_params=pltpu.CompilerParams(vmem_limit_bytes=ADD_LIMIT),
     )(tags, up, down, coarse)
 
 

time: 102 us -> 97.6 us (0.957)
  waiting for transfers between devices: 9.97 us -> 0.01 us
  Pallas kernels: 79.5 us -> 84.2 us
  local copies, waits for them, and re-layouts: 3.81 us -> 6.3 us
  other arithmetic: 2.02 us -> 0 us
    ppermute x2, waiting for transfers between devices: 9.97 us -> 0.01 us  [passed_along(): return lax.ppermute(block, axis, route)]
    pallas_call x1, Pallas kernels: 45.6 us -> 54.5 us  [local(): pl.pallas_call(lambda *r: front_kernel(capacity, *r), out_shape=[jax.Shap...]
    unnamed x4 -> x24, local copies, waits for them, and re-layouts: 0.95 us -> 6.3 us
    pallas_call x1, Pallas kernels: 5.81 us -> 3.59 us  [local(): pl.pallas_call(lambda *r: add_kernel(capacity, *r), out_shape=jax.ShapeDt...]
    concatenate x2 -> x0, local copies, waits for them, and re-layouts: 2.15 us -> none  [local(): jnp.concatenate([a_cols, ap_slot.reshape(rows_here, 14), p_aggs % CR_DEV,...]
    pallas_call x1, Pallas kernels: 28.1 us -> 26.1 us  [local(): pl.pallas_call(lambda *r: main_kernel(capacity, *r), out_shape=[jax.Shape...]
  transfers between devices with their start and end apart: 2 -> 2, of which waited for: 2 -> 0; matrix products, arithmetic and copies ran while one was open for 1% -> 0% of each run, Pallas kernels for 28% -> 27%
where the time goes in v3:
time: 97.6 us; the launch traced here: 96.8 us
  Pallas kernels  84.2 us (86%)
  local copies, waits for them, and re-layouts  6.3 us (6%)
  starting transfers between devices  6.18 us (6%)
    pallas_call x1, Pallas kernels, local(): pl.pallas_call(lambda *r: front_kernel(capacity, *r), out_shape=[jax.Shap...  54.5 us
    pallas_call x1, Pallas kernels, local(): pl.pallas_call(lambda *r: main_kernel(capacity, *r), out_shape=[jax.Shape...  26.1 us
    unnamed x24, local copies, waits for them, and re-layouts  6.3 us
    ppermute x2, starting transfers between devices, passed_along(): return lax.ppermute(block, axis, route)  6.18 us
    pallas_call x1, Pallas kernels, local(): pl.pallas_call(lambda *r: add_kernel(capacity, *r), out_shape=jax.ShapeDt...  3.59 us
  transfers between devices with their start and end apart: 2, of which 0 were waited for; matrix products, arithmetic and copies ran while one was open for 0% of the time, Pallas kernels for 27%

profile of v3, /device:TPU:13, one launch (start us, length us, event | category | flops | bytes accessed | tf_op | source)
XLA Modules:
  0.0 96.8 jit_solution(7065017361558657123)
XLA Ops:
  0.0 0.0 copy-start
  0.0 0.0 copy-start.1
  0.0 0.0 copy-start.2
  0.0 0.0 copy-start.3
  0.0 0.0 copy-start.4
  0.0 54.5 %shard_map.73 = (bf16[32,2,128,128]{3,2,1,0:T(8,128)(2,1)}, bf16[4,4,128,128]{3,2,1,0:T(8,128)(2,1)}, bf16[4,4,128,128]{3,2,1,0:T(8,128)(2,1)}, s32[2,72]{1,0:T(...) custom-call(s32[7,72]{1,0:T(8,128)} %bitcast.6, ...), custom_call_target="tpu_custom_call" | custom-call | flops 1358954496 | bytes 25000000 | tf_op jit(solution)/shard_map/pallas_call | solution.py:345
  54.5 3.2 %collective-permute-start = (bf16[5,4,128,128]{3,2,1,0:T(8,128)(2,1)}, bf16[5,4,128,128]{3,2,1,0:T(8,128)(2,1)S(1)}, u32[]{:S(2)}, u32[]{:S(2)}) collective-permute-start(bf16[5,4,128,128]{3,2,1,0:T(8,128)(2,1)} %get-tuple-element.24), channel_id=1, source_target_pairs={{0,4},{4,8},{8,12},{12,16},{16,20},{20,24},{24,28},{1,5},{5,9},{9,... | collective-permute-start | bytes 1966088 | tf_op jit(solution)/shard_map/ppermute | solution.py:28
  57.7 2.9 %collective-permute-start.1 = (bf16[5,4,128,128]{3,2,1,0:T(8,128)(2,1)}, bf16[5,4,128,128]{3,2,1,0:T(8,128)(2,1)S(1)}, u32[]{:S(2)}, u32[]{:S(2)}) collective-permute-start(bf16[5,4,128,128]{3,2,1,0:T(8,128)(2,1)} %get-tuple-element.25), channel_id=1, source_target_pairs={{4,0},{8,4},{12,8},{16,12},{20,16},{24,20},{28,24},{5,1},{9,5},{13... | collective-permute-start | bytes 1966088 | tf_op jit(solution)/shard_map/ppermute | solution.py:28
  60.7 0.0 copy-done
  60.7 0.0 copy-done.1
  60.7 0.0 copy-done.2
  60.7 0.0 copy-done.3
  60.7 0.0 copy-done.4
  60.7 0.0 copy-start.5
  60.7 1.6 %copy-done.5 = bf16[32,2,128,128]{3,2,1,0:T(8,128)(2,1)S(1)} copy-done((bf16[32,2,128,128]{3,2,1,0:T(8,128)(2,1)S(1)}, bf16[32,2,128,128]{3,2,1,0:T(8,128)(2,1)}, u32[]{:S(2)}) %copy-start.5) | copy-done | bytes 2097176
  62.3 0.0 copy-start.6
  62.3 1.0 %copy-done.6 = bf16[4,4,128,128]{3,2,1,0:T(8,128)(2,1)S(1)} copy-done((bf16[4,4,128,128]{3,2,1,0:T(8,128)(2,1)S(1)}, bf16[4,4,128,128]{3,2,1,0:T(8,128)(2,1)}, u32[]{:S(2)}) %copy-start.6) | copy-done | bytes 524312
  63.4 0.0 copy-start.7
  63.4 1.0 %copy-done.7 = bf16[4,4,128,128]{3,2,1,0:T(8,128)(2,1)S(1)} copy-done((bf16[4,4,128,128]{3,2,1,0:T(8,128)(2,1)S(1)}, bf16[4,4,128,128]{3,2,1,0:T(8,128)(2,1)}, u32[]{:S(2)}) %copy-start.7) | copy-done | bytes 524312
  64.4 0.0 copy-start.8
  64.4 0.7 copy-done.8
  65.1 0.0 copy-start.9
  65.1 0.7 copy-done.9
  65.8 0.0 copy-start.10
  65.8 0.7 copy-done.10
  66.4 0.0 copy-start.11
  66.4 0.6 copy-done.11
  67.0 26.1 %shard_map.74 = (f32[65,128,128]{2,1,0:T(8,128)S(1)}, s32[18,5]{1,0:T(8,128)S(1)}) custom-call(s32[7,72]{1,0:T(8,128)S(1)} %bitcast.7, s32[7,2,72]{2,1,0:T(2,128)S(1)} %bitcast.5, s32[2,72]{1,0:T(2,128)S(1)} %bitcast.12, s32[2,4,72]{2,1,0:T(4,128)S(1)} %bitcast.9, s32[2,72]{1,0:T(2,128)S(1)} %copy-done.10, s32[2,72]{1,0:T(2,128)S(1)} %copy-done.11, ...), custom_call_target="tpu_custom_call" | custom-call | flops 6643777536 | bytes 26000000 | tf_op jit(solution)/shard_map/pallas_call | solution.py:383
  93.2 0.0 collective-permute-done.r_1_
  93.2 0.0 collective-permute-done.1.r_2_
  93.2 3.6 %shard_map.75 = f32[4,16,128,128]{3,2,1,0:T(8,128)} custom-call(s32[18,5]{1,0:T(8,128)S(1)} %get-tuple-element.23.r_0_, bf16[5,4,128,128]{3,2,1,0:T(8,128)(2,1)S(1)} %collective-permute-done.r_1_, bf16[5,4,128,128]{3,2,1,0:T(8,128)(2,1)S(1)} %collective-permute-done.1.r_2_, f32[65,128,128]{2,1,0:T(8,128)S(1)} %get-tuple-element.26.r_3_), custom_call_target="tpu_custom_call" | custom-call | tf_op jit(solution)/shard_map/pallas_call | solution.py:409
Async XLA Ops:
  0.0 60.7 %copy-start = (bf16[72,2,128,128]{3,2,1,0:T(8,128)(2,1)S(1)}, bf16[72,2,128,128]{3,2,1,0:T(8,128)(2,1)}, u32[]{:S(2)}) copy-start(bf16[72,2,128,128]{3,2,1,0:T(8,128)(2,1)} %r_9_.1) | copy-start | bytes 14155780
  0.0 60.7 %copy-start.1 = (s32[72,7,2]{0,2,1:T(2,128)S(1)}, s32[72,7,2]{0,2,1:T(2,128)}, u32[]{:S(2)}) copy-start(s32[72,7,2]{0,2,1:T(2,128)} %param.9) | copy-start | bytes 12100
  0.0 60.7 %copy-start.2 = (s32[72,7]{0,1:T(8,128)S(1)}, s32[72,7]{0,1:T(8,128)}, u32[]{:S(2)}) copy-start(s32[72,7]{0,1:T(8,128)} %param.8) | copy-start | bytes 6052
  0.0 60.7 %copy-start.3 = (s32[72,2,4]{0,2,1:T(4,128)S(1)}, s32[72,2,4]{0,2,1:T(4,128)}, u32[]{:S(2)}) copy-start(s32[72,2,4]{0,2,1:T(4,128)} %param.12) | copy-start | bytes 6916
  0.0 60.7 %copy-start.4 = (s32[72,2]{0,1:T(2,128)S(1)}, s32[72,2]{0,1:T(2,128)}, u32[]{:S(2)}) copy-start(s32[72,2]{0,1:T(2,128)} %param.11) | copy-start | bytes 1732
  54.5 38.7 %collective-permute-start = (bf16[5,4,128,128]{3,2,1,0:T(8,128)(2,1)}, bf16[5,4,128,128]{3,2,1,0:T(8,128)(2,1)S(1)}, u32[]{:S(2)}, u32[]{:S(2)}) collective-permute-start(bf16[5,4,128,128]{3,2,1,0:T(8,128)(2,1)} %get-tuple-element.24), channel_id=1, source_target_pairs={{0,4},{4,8},{8,12},{12,16},{16,20},{20,24},{24,28},{1,5},{5,9},{9,... | collective-permute-start | bytes 1966088 | tf_op jit(solution)/shard_map/ppermute | solution.py:28
  57.7 35.5 %collective-permute-start.1 = (bf16[5,4,128,128]{3,2,1,0:T(8,128)(2,1)}, bf16[5,4,128,128]{3,2,1,0:T(8,128)(2,1)S(1)}, u32[]{:S(2)}, u32[]{:S(2)}) collective-permute-start(bf16[5,4,128,128]{3,2,1,0:T(8,128)(2,1)} %get-tuple-element.25), channel_id=1, source_target_pairs={{4,0},{8,4},{12,8},{16,12},{20,16},{24,20},{28,24},{5,1},{9,5},{13... | collective-permute-start | bytes 1966088 | tf_op jit(solution)/shard_map/ppermute | solution.py:28
  60.7 1.6 %copy-start.5 = (bf16[32,2,128,128]{3,2,1,0:T(8,128)(2,1)S(1)}, bf16[32,2,128,128]{3,2,1,0:T(8,128)(2,1)}, u32[]{:S(2)}) copy-start(bf16[32,2,128,128]{3,2,1,0:T(8,128)(2,1)} %get-tuple-element.20.r_10_) | copy-start | bytes 6291460
  62.3 1.0 %copy-start.6 = (bf16[4,4,128,128]{3,2,1,0:T(8,128)(2,1)S(1)}, bf16[4,4,128,128]{3,2,1,0:T(8,128)(2,1)}, u32[]{:S(2)}) copy-start(bf16[4,4,128,128]{3,2,1,0:T(8,128)(2,1)} %get-tuple-element.21.r_11_) | copy-start | bytes 1572868
  63.4 1.0 %copy-start.7 = (bf16[4,4,128,128]{3,2,1,0:T(8,128)(2,1)S(1)}, bf16[4,4,128,128]{3,2,1,0:T(8,128)(2,1)}, u32[]{:S(2)}) copy-start(bf16[4,4,128,128]{3,2,1,0:T(8,128)(2,1)} %get-tuple-element.22.r_12_) | copy-start | bytes 1572868
  64.4 0.7 copy-start.8
  65.1 0.7 copy-start.9
  65.8 0.7 copy-start.10
  66.4 0.6 copy-start.11

commit v4 on v3

--- a/solution.py
+++ b/solution.py
@@ -16,9 +16,10 @@
 DMA = pltpu.SemaphoreType.DMA
 MESH = pl.DeviceIdType.MESH
 VMEM_LIMIT = 56 * 1024 * 1024
-MAIN_LIMIT = 32 * 1024 * 1024
+MAIN_LIMIT = 56 * 1024 * 1024
 ADD_LIMIT = 20 * 1024 * 1024
-EARLY = 4
+EARLY = 3
+GROUP = 3
 TOGETHER = 4
 
 
@@ -168,9 +169,9 @@
     ghost_copy.start()
     pall[pl.ds(rows_here, 4 * sends)] = land[...]
 
-    def products(m, places):
+    def products(places):
         strips = []
-        lines = [rows[m], rows[capacity + m]]
+        lines = [line for line, _, _ in places]
         for side, i in enumerate(lines):
             for k in range(7):
                 v = cols[k, i]
@@ -192,7 +193,7 @@
             strips.append(jnp.concatenate(chunks, axis=0))
         for side, i in enumerate(lines):
             part = fold(pall[i, 1], strips[side])
-            out, place = places[side]
+            _, out, place = places[side]
             for s in range(4):
                 out[place, s] = part[:, 128 * s : 128 * (s + 1)].astype(jnp.bfloat16)
 
@@ -202,21 +203,29 @@
             (remote(9 + 2 * m, box_down.at[m], early_down.at[m], 1), 1),
         ]
 
-    def early_step(m, carry):
-        products(m, ((box_up, m), (box_down, m)))
-        start(early_pairs(m))
-        return carry
-
-    def late_step(m, carry):
-        products(m, ((late_up, m - EARLY), (late_down, m - EARLY)))
+    def group(first, size, up, down, skipped):
+        places = []
+        for n in range(size):
+            m = first + n
+            places.append((rows[m], up, m - skipped))
+            places.append((rows[capacity + m], down, m - skipped))
+        products(places)
+
+    def late_step(n, carry):
+        group(EARLY + n * GROUP, GROUP, late_up, late_down, EARLY)
         return carry
 
     def early_end(m, carry):
         finish(early_pairs(m))
         return carry
 
-    lax.fori_loop(0, EARLY, early_step, 0)
-    lax.fori_loop(EARLY, capacity, late_step, 0)
+    group(0, EARLY, box_up, box_down, 0)
+    for m in range(EARLY):
+        start(early_pairs(m))
+    steps, rest = divmod(capacity - EARLY, GROUP)
+    lax.fori_loop(0, steps, late_step, 0)
+    if rest:
+        group(capacity - rest, rest, late_up, late_down, EARLY)
     ghost_copy.wait()
     lax.fori_loop(0, EARLY, early_end, 0)
 
@@ -364,7 +373,7 @@
             VMEM((4 * sends, 2, tile, tile), bf16),
             VMEM((EARLY, 4, tile, tile), bf16),
             VMEM((EARLY, 4, tile, tile), bf16),
-            VMEM((2, 7, tile, 2 * tile), jnp.float32),
+            VMEM((2 * GROUP, 7, tile, 2 * tile), jnp.float32),
             SMEM((2 * capacity,), jnp.int32),
             DMA((3,)),
             DMA((8 + 2 * EARLY,)),

time: 97.6 us -> 96.3 us (0.987)
  waiting for transfers between devices: 0.01 us -> 6.17 us
  Pallas kernels: 84.2 us -> 80.6 us
  local copies, waits for them, and re-layouts: 6.3 us -> 2.91 us
    ppermute x2, waiting for transfers between devices: 0.01 us -> 6.17 us  [passed_along(): return lax.ppermute(block, axis, route)]
    pallas_call x1, Pallas kernels: 54.5 us -> 50 us  [local(): pl.pallas_call(lambda *r: front_kernel(capacity, *r), out_shape=[jax.Shap...]
    unnamed x24 -> x4, local copies, waits for them, and re-layouts: 6.3 us -> 2.91 us
  transfers between devices with their start and end apart: 2 -> 2, of which waited for: 0 -> 2; matrix products, arithmetic and copies ran while one was open for 0% -> 0% of each run, Pallas kernels for 27% -> 28%
where the time goes in v4:
time: 96.3 us; the launch traced here: 95.9 us
  Pallas kernels  80.6 us (84%)
  starting transfers between devices  6.18 us (6%)
  waiting for transfers between devices  6.17 us (6%)
  local copies, waits for them, and re-layouts  2.91 us (3%)
    pallas_call x1, Pallas kernels, local(): pl.pallas_call(lambda *r: front_kernel(capacity, *r), out_shape=[jax.Shap...  50 us
    pallas_call x1, Pallas kernels, local(): pl.pallas_call(lambda *r: main_kernel(capacity, *r), out_shape=[jax.Shape...  26.9 us
    ppermute x2, starting transfers between devices, passed_along(): return lax.ppermute(block, axis, route)  6.18 us
    ppermute x2, waiting for transfers between devices, passed_along(): return lax.ppermute(block, axis, route)  6.17 us
    pallas_call x1, Pallas kernels, local(): pl.pallas_call(lambda *r: add_kernel(capacity, *r), out_shape=jax.ShapeDt...  3.65 us
    unnamed x4, local copies, waits for them, and re-layouts  2.91 us
  transfers between devices with their start and end apart: 2, of which 2 were waited for; matrix products, arithmetic and copies ran while one was open for 0% of the time, Pallas kernels for 28%

profile of v4, /device:TPU:13, one launch (start us, length us, event | category | flops | bytes accessed | tf_op | source)
XLA Modules:
  0.0 95.9 jit_solution(1979904008187625097)
XLA Ops:
  0.0 50.0 %shard_map.73 = (bf16[32,2,128,128]{3,2,1,0:T(8,128)(2,1)}, bf16[3,4,128,128]{3,2,1,0:T(8,128)(2,1)}, bf16[3,4,128,128]{3,2,1,0:T(8,128)(2,1)}, s32[2,72]{1,0:T(...) custom-call(s32[7,72]{1,0:T(8,128)} %bitcast.6, ...), custom_call_target="tpu_custom_call" | custom-call | flops 1358954496 | bytes 25000000 | tf_op jit(solution)/shard_map/pallas_call | solution.py:354
  50.0 3.2 %collective-permute-start = (bf16[6,4,128,128]{3,2,1,0:T(8,128)(2,1)}, bf16[6,4,128,128]{3,2,1,0:T(8,128)(2,1)S(1)}, u32[]{:S(2)}, u32[]{:S(2)}) collective-permute-start(bf16[6,4,128,128]{3,2,1,0:T(8,128)(2,1)} %get-tuple-element.24), channel_id=1, source_target_pairs={{0,4},{4,8},{8,12},{12,16},{16,20},{20,24},{24,28},{1,5},{5,9},{9,... | collective-permute-start | bytes 2359304 | tf_op jit(solution)/shard_map/ppermute | solution.py:29
  53.2 2.9 %collective-permute-start.1 = (bf16[6,4,128,128]{3,2,1,0:T(8,128)(2,1)}, bf16[6,4,128,128]{3,2,1,0:T(8,128)(2,1)S(1)}, u32[]{:S(2)}, u32[]{:S(2)}) collective-permute-start(bf16[6,4,128,128]{3,2,1,0:T(8,128)(2,1)} %get-tuple-element.25), channel_id=1, source_target_pairs={{4,0},{8,4},{12,8},{16,12},{20,16},{24,20},{28,24},{5,1},{9,5},{13... | collective-permute-start | bytes 2359304 | tf_op jit(solution)/shard_map/ppermute | solution.py:29
  56.2 26.9 %shard_map.74 = (f32[65,128,128]{2,1,0:T(8,128)}, s32[18,5]{1,0:T(8,128)}) custom-call(s32[7,72]{1,0:T(8,128)} %bitcast.7, s32[7,2,72]{2,1,0:T(2,128)} %bitcast.5, s32[2,72]{1,0:T(2,128)} %bitcast.12, s32[2,4,72]{2,1,0:T(4,128)} %bitcast.9, s32[2,72]{1,0:T(2,128)} %get-tuple-element.16.r_4_, s32[2,72]{1,0:T(2,128)} %get-tuple-element.17.r_5_, ...), custom_call_target="tpu_custom_call" | custom-call | flops 6643777536 | bytes 26000000 | tf_op jit(solution)/shard_map/pallas_call | solution.py:392
  83.1 2.9 %collective-permute-done.r_1_ = bf16[6,4,128,128]{3,2,1,0:T(8,128)(2,1)S(1)} collective-permute-done((bf16[6,4,128,128]{3,2,1,0:T(8,128)(2,1)}, bf16[6,4,128,128]{3,2,1,0:T(8,128)(2,1)S(1)}, u32[]{:S(2)}, u32[]{:S(2)}) %collective-permute-start) | collective-permute-done | bytes 786464 | tf_op jit(solution)/shard_map/ppermute | solution.py:29
  86.1 3.2 %collective-permute-done.1.r_2_ = bf16[6,4,128,128]{3,2,1,0:T(8,128)(2,1)S(1)} collective-permute-done((bf16[6,4,128,128]{3,2,1,0:T(8,128)(2,1)}, bf16[6,4,128,128]{3,2,1,0:T(8,128)(2,1)S(1)}, u32[]{:S(2)}, u32[]{:S(2)}) %collective-permute-start.1) | collective-permute-done | bytes 786464 | tf_op jit(solution)/shard_map/ppermute | solution.py:29
  89.3 0.0 copy-start
  89.3 2.2 %copy-done = f32[65,128,128]{2,1,0:T(8,128)S(1)} copy-done((f32[65,128,128]{2,1,0:T(8,128)S(1)}, f32[65,128,128]{2,1,0:T(8,128)}, u32[]{:S(2)}) %copy-start) | copy-done | bytes 4259864
  91.5 0.0 copy-start.1
  91.5 0.7 copy-done.1
  92.2 3.7 %shard_map.75 = f32[4,16,128,128]{3,2,1,0:T(8,128)} custom-call(s32[18,5]{1,0:T(8,128)S(1)} %copy-done.1, bf16[6,4,128,128]{3,2,1,0:T(8,128)(2,1)S(1)} %collective-permute-done.r_1_, bf16[6,4,128,128]{3,2,1,0:T(8,128)(2,1)S(1)} %collective-permute-done.1.r_2_, f32[65,128,128]{2,1,0:T(8,128)S(1)} %copy-done), custom_call_target="tpu_custom_call" | custom-call | tf_op jit(solution)/shard_map/pallas_call | solution.py:418
Async XLA Ops:
  50.0 36.1 %collective-permute-start = (bf16[6,4,128,128]{3,2,1,0:T(8,128)(2,1)}, bf16[6,4,128,128]{3,2,1,0:T(8,128)(2,1)S(1)}, u32[]{:S(2)}, u32[]{:S(2)}) collective-permute-start(bf16[6,4,128,128]{3,2,1,0:T(8,128)(2,1)} %get-tuple-element.24), channel_id=1, source_target_pairs={{0,4},{4,8},{8,12},{12,16},{16,20},{20,24},{24,28},{1,5},{5,9},{9,... | collective-permute-start | bytes 2359304 | tf_op jit(solution)/shard_map/ppermute | solution.py:29
  53.2 36.1 %collective-permute-start.1 = (bf16[6,4,128,128]{3,2,1,0:T(8,128)(2,1)}, bf16[6,4,128,128]{3,2,1,0:T(8,128)(2,1)S(1)}, u32[]{:S(2)}, u32[]{:S(2)}) collective-permute-start(bf16[6,4,128,128]{3,2,1,0:T(8,128)(2,1)} %get-tuple-element.25), channel_id=1, source_target_pairs={{4,0},{8,4},{12,8},{16,12},{20,16},{24,20},{28,24},{5,1},{9,5},{13... | collective-permute-start | bytes 2359304 | tf_op jit(solution)/shard_map/ppermute | solution.py:29
  89.3 2.2 %copy-start = (f32[65,128,128]{2,1,0:T(8,128)S(1)}, f32[65,128,128]{2,1,0:T(8,128)}, u32[]{:S(2)}) copy-start(f32[65,128,128]{2,1,0:T(8,128)} %get-tuple-element.26.r_3_) | copy-start | bytes 12779524
  91.5 0.7 copy-start.1
